TPU v7x, 32 devices: a whole 2x2x4 slice. The times are simulated.
32 devices in a mesh: seq: 4 (over z), tensor: 8 (over y, x, core).
Axes of the slice: x: 2, y: 2, z: 4, core: 2. Of those that a mesh axis runs over, the one named last changes fastest.
Arguments:
- hidden: bfloat16 [4, 128, 8192], P('seq', None, 'tensor'), may hold values from -2.5 to 2.5
- neighbours: bfloat16 [4, 8, 128, 1024], P('seq', 'tensor'), may hold values from -2.5 to 2.5
- slot_of: int32 [4, 2, 2], P('seq'), may hold values from 0 to 7, as said below
- w_query: bfloat16 [8192, 8192], P(None, 'tensor'), may hold values from -0.0625 to 0.0625
- w_key: bfloat16 [1024, 8192], P(None, 'tensor'), may hold values from -0.1875 to 0.1875
- w_value: bfloat16 [1024, 8192], P(None, 'tensor'), may hold values from -0.1875 to 0.1875
- out_grad: bfloat16 [4, 128, 8192], P('seq', None, 'tensor'), may hold values from -4 to 4
Outputs:
- attended: bfloat16 [4, 128, 8192], P('seq', None, 'tensor')
- hidden_grad: bfloat16 [4, 128, 8192], P('seq', None, 'tensor')
- neighbour_grad: bfloat16 [4, 8, 128, 1024], P('seq', 'tensor')
- query_weight_grad: float32 [8192, 8192], P('seq', 'tensor')
- key_weight_grad: float32 [1024, 8192], P('seq', 'tensor')
- value_weight_grad: float32 [1024, 8192], P('seq', 'tensor')
Inputs may be any that keep to these rules, and one draw needn't show every extreme that they name: `slot_of`: slot j of a sequence's group is slot j % 1 of tensor device j; the 4 entries of one sequence are distinct.
All inputs are finite; a program needn't handle non-finite values.
Results may differ from a plain program's by a relative error of at most 0.013.
Values may be sent and summed in bfloat16 or wider, within the bound.
A program may use at most 192 MiB of HBM per device.

v0:
```python
import math

import jax
import jax.numpy as jnp
from jax import lax
from jax.sharding import PartitionSpec as P

HS = 128
DE = 1024
SPAN = 64
R = 128


def contract_rows(left, right):
    return lax.dot_general(
        left, right, (((0,), (0,)), ((), ())), preferred_element_type=jnp.float32
    )


def contract_cols(left, right):
    return lax.dot_general(
        left, right, (((1,), (1,)), ((), ())), preferred_element_type=jnp.float32
    )


def body(hidden, neighbours, slot_of, w_query, w_key, w_value, out_grad):
    width = w_query.shape[1]
    heads_here = width // HS
    slot_count = neighbours.shape[1]
    span_count = slot_of.shape[1]
    lag = SPAN - 1
    scale = 1.0 / math.sqrt(HS)
    whole = lax.all_gather(hidden, "tensor", axis=2, tiled=True)[0]
    length = whole.shape[0]
    query = jnp.dot(whole, w_query, preferred_element_type=jnp.float32).astype(jnp.bfloat16)
    slots = slot_of[0].reshape(-1)
    every = lax.all_gather(neighbours, "tensor", axis=1, tiled=True)[0]
    picked = jnp.take(every, slots, axis=0)
    states = picked.reshape(-1, DE)
    keys = jnp.dot(states, w_key, preferred_element_type=jnp.float32).astype(jnp.bfloat16)
    values = jnp.dot(states, w_value, preferred_element_type=jnp.float32).astype(jnp.bfloat16)
    shaped_keys = keys.reshape(span_count, -1, heads_here, HS)
    shaped_values = values.reshape(span_count, -1, heads_here, HS)
    blank = jnp.zeros((lag, width), jnp.bfloat16)
    shifted = jnp.concatenate([query[lag:], blank], 0).reshape(span_count, SPAN, heads_here, HS)
    grads = jnp.concatenate([out_grad[0][lag:], blank], 0).reshape(span_count, SPAN, heads_here, HS)
    scores = (
        jnp.einsum("uqhd,ukhd->uhqk", shifted, shaped_keys, preferred_element_type=jnp.float32)
        * scale
    )
    raised = jnp.exp(scores)
    shares = raised / jnp.sum(raised, axis=-1, keepdims=True)
    share_bf = shares.astype(jnp.bfloat16)
    mixed = jnp.einsum(
        "uhqk,ukhd->uqhd", share_bf, shaped_values, preferred_element_type=jnp.float32
    ).astype(jnp.bfloat16)
    attended = jnp.concatenate([blank, mixed.reshape(length, width)[: length - lag]], 0)[None]
    share_grad = jnp.einsum(
        "uqhd,ukhd->uhqk", grads, shaped_values, preferred_element_type=jnp.float32
    )
    centre = jnp.sum(shares * share_grad, axis=-1, keepdims=True)
    score_grad = (shares * (share_grad - centre) * scale).astype(jnp.bfloat16)
    shift_grad = jnp.einsum(
        "uhqk,ukhd->uqhd", score_grad, shaped_keys, preferred_element_type=jnp.float32
    ).astype(jnp.bfloat16)
    key_grad = (
        jnp.einsum("uhqk,uqhd->ukhd", score_grad, shifted, preferred_element_type=jnp.float32)
        .astype(jnp.bfloat16)
        .reshape(-1, width)
    )
    value_grad = (
        jnp.einsum("uhqk,uqhd->ukhd", share_bf, grads, preferred_element_type=jnp.float32)
        .astype(jnp.bfloat16)
        .reshape(-1, width)
    )
    query_grad = jnp.concatenate([blank, shift_grad.reshape(length, width)[: length - lag]], 0)
    feature_grad = lax.psum_scatter(
        contract_cols(w_query, query_grad).astype(jnp.bfloat16),
        "tensor",
        scatter_dimension=0,
        tiled=True,
    ).astype(jnp.float32)
    hidden_grad = feature_grad.T.astype(jnp.bfloat16)[None]
    local_term = contract_cols(key_grad, w_key) + contract_cols(value_grad, w_value)
    flat_bf = local_term.astype(jnp.bfloat16).reshape(slots.shape[0], -1)
    wanted = lax.iota(jnp.int32, slot_count * lax.axis_size("tensor"))
    select = (wanted[:, None] == slots[None, :]).astype(jnp.bfloat16)
    placed = lax.psum_scatter(
        jnp.dot(select, flat_bf, preferred_element_type=jnp.float32).astype(jnp.bfloat16),
        "tensor",
        scatter_dimension=0,
        tiled=True,
    )
    neighbour_grad = placed.reshape(1, slot_count, R, DE)
    query_part = contract_rows(whole, query_grad)
    key_part = contract_rows(states, key_grad)
    value_part = contract_rows(states, value_grad)
    summed = (
        lax.psum_scatter(
            query_part.astype(jnp.bfloat16), "seq", scatter_dimension=0, tiled=True
        ).astype(jnp.float32),
        lax.psum_scatter(
            key_part.astype(jnp.bfloat16), "seq", scatter_dimension=0, tiled=True
        ).astype(jnp.float32),
        lax.psum_scatter(
            value_part.astype(jnp.bfloat16), "seq", scatter_dimension=0, tiled=True
        ).astype(jnp.float32),
    )
    return (attended, hidden_grad, neighbour_grad, summed[0], summed[1], summed[2])


def solution(mesh):
    return jax.shard_map(
        body,
        mesh=mesh,
        in_specs=(
            P("seq", None, "tensor"),
            P("seq", "tensor", None, None),
            P("seq", None, None),
            P(None, "tensor"),
            P(None, "tensor"),
            P(None, "tensor"),
            P("seq", None, "tensor"),
        ),
        out_specs=(
            P("seq", None, "tensor"),
            P("seq", None, "tensor"),
            P("seq", "tensor", None, None),
            P("seq", "tensor"),
            P("seq", "tensor"),
            P("seq", "tensor"),
        ),
        check_vma=False,
    )
```

profile of v0, /device:TPU:0, one launch (start us, length us, event | category | flops | bytes accessed | tf_op | source)
XLA Modules:
  0.0 588.7 jit_solution(10083463046167378192)
XLA Ops:
  7.2 0.0 all-gather.5.cloned.1.call-start
  7.2 0.7 all-gather.5.cloned.1.call-update
  7.9 0.0 all-gather.3.cloned.1.call-start
  8.0 0.7 all-gather.3.cloned.1.call-update
  8.7 0.0 all-reduce.7.cloned.1.call-start
  8.7 0.8 reshape_squeeze.5
  9.5 0.8 reshape_squeeze.6
  10.2 0.9 slice_bitcast_fusion
  11.2 0.8 copy.51
  12.0 0.1 broadcast_bitcast_fusion
  12.1 28.5 %all-gather.5.cloned.1.call-done = bf16[1,128,8192]{2,1,0:T(8,128)(2,1)} async-done(((bf16[1,128,1024]{2,1,0:T(8,128)(2,1)}), bf16[1,128,8192]{2,1,0:T(8,128)(2,1)}) %all-gather.5.cloned.1.call-update) | async-done | bytes 2097168 | tf_op jit(solution)/shard_map/all_gather | solution.py:33
  40.6 8.7 %fusion.3 = bf16[128,1024]{1,0:T(8,128)(2,1)S(1)} fusion(bf16[8192,1024]{1,0:T(8,128)(2,1)} %param.10, bf16[1,128,8192]{2,1,0:T(8,128)(2,1)} %all-gather.5.cloned.1.call-done), kind=kOutput, calls=%fused_computation.7 | convolution fusion | flops 2147483648 | bytes 19136512 | tf_op jit(solution)/shard_map/dot_general | solution.py:35
  49.4 20.9 %all-gather.3.cloned.1.call-done = bf16[1,8,128,1024]{3,2,0,1:T(8,128)(2,1)} async-done(((bf16[1,1,128,1024]{3,2,0,1:T(8,128)(2,1)}), bf16[1,8,128,1024]{3,2,0,1:T(8,128)(2,1)}) %all-gather.3.cloned.1.call-update) | async-done | bytes 2097168 | tf_op jit(solution)/shard_map/all_gather | solution.py:37
  70.4 2.2 gather_fusion
  72.6 0.2 bitcast_select_fusion
  72.8 1.3 fusion.6
  74.1 0.3 copy-done.10
  74.4 1.3 fusion.5
  75.7 1.3 copy.49
  76.9 0.3 copy.48
  77.2 0.5 fusion.12
  77.7 1.0 copy-done.6
  78.7 1.2 fusion.35
  79.9 3.3 fusion.8
  83.2 2.8 fusion.29
  85.9 3.8 fusion.7
  89.8 2.4 copy.43
  92.2 2.5 copy.45
  94.6 2.7 fusion.19
  97.3 1.3 add_convert_fusion
  98.6 0.8 reshape.145
  99.4 2.0 convolution_convert_fusion
  101.4 0.0 all-reduce.7.cloned.1.call-update
  101.5 0.2 reduce-scatter.11.cloned.1.call-start
  101.7 0.2 broadcast_select_fusion
  101.9 0.8 copy-done.9
  102.7 2.6 convolution_convert_fusion.2
  105.3 0.0 reduce-scatter.11.cloned.1.call-update
  105.3 0.0 reduce-scatter.9.cloned.1.call-start
  105.4 1.1 copy-done.7
  106.5 2.7 convolution_convert_fusion.3
  109.2 0.0 reduce-scatter.9.cloned.1.call-update
  109.2 0.0 reduce-scatter.7.cloned.1.call-start
  109.3 1.1 copy-done.5
  110.4 2.7 fusion.15
  113.1 0.2 copy.41
  113.4 8.3 %convert_bitcast_fusion = bf16[8192,1024]{0,1:T(8,128)(2,1)} fusion(bf16[1,128,8192]{2,1,0:T(8,128)(2,1)S(1)} %copy-done.2, bf16[65,1024]{1,0:T(8,128)(2,1)S(1)} %slice.24), kind=kOutput, calls=%fused_computation.3 | convolution fusion | flops 2155872256 | bytes 19007488 | tf_op jit(solution)/shard_map/dot_general | solution.py:15
  121.7 0.0 reduce-scatter.5.cloned.1.call-start
  121.7 12.8 %fusion.1 = bf16[8192,128]{0,1:T(8,128)(2,1)} fusion(bf16[8192,1024]{1,0:T(8,128)(2,1)} %param.10, bf16[65,1024]{1,0:T(8,128)(2,1)S(1)} %slice.24), kind=kOutput, calls=%fused_computation.5 | convolution fusion | flops 2148532224 | bytes 19007488 | tf_op jit(solution)/shard_map/dot_general | solution.py:21
  134.5 0.6 copy-done.12
  135.2 0.6 dynamic-slice
  135.7 2.1 fusion.14
  137.8 0.2 copy.37
  138.1 0.7 pad_bitcast_fusion.1
  138.8 24.2 %all-reduce.7.cloned.1.call-done = bf16[8,131072]{1,0:T(8,128)(2,1)} async-done(((bf16[8,131072]{1,0:T(8,128)(2,1)}), bf16[8,131072]{1,0:T(8,128)(2,1)}) %all-reduce.7.cloned.1.call-update) | async-done | bytes 2097168
  163.1 3.8 dynamic-slice_reduce_fusion
  166.9 0.8 reshape.146
  167.7 40.6 %reduce-scatter.11.cloned.1.call-done = bf16[256,1024]{1,0:T(8,128)(2,1)} async-done(((bf16[1024,1024]{1,0:T(8,128)(2,1)}), bf16[256,1024]{1,0:T(8,128)(2,1)}) %reduce-scatter.11.cloned.1.call-update) | async-done | bytes 524304 | tf_op jit(solution)/shard_map/reduce_scatter | solution.py:105
  208.3 2.1 convert_element_type.102
  210.4 43.3 %reduce-scatter.9.cloned.1.call-done = bf16[256,1024]{1,0:T(8,128)(2,1)} async-done(((bf16[1024,1024]{1,0:T(8,128)(2,1)}), bf16[256,1024]{1,0:T(8,128)(2,1)}) %reduce-scatter.9.cloned.1.call-update) | async-done | bytes 524304 | tf_op jit(solution)/shard_map/reduce_scatter | solution.py:102
  253.8 2.1 convert_element_type.100
  255.9 279.8 %reduce-scatter.7.cloned.1.call-done = bf16[2048,1024]{0,1:T(8,128)(2,1)} async-done(((bf16[8192,1024]{0,1:T(8,128)(2,1)}), bf16[2048,1024]{0,1:T(8,128)(2,1)}) %reduce-scatter.7.cloned.1.call-update) | async-done | bytes 4194320 | tf_op jit(solution)/shard_map/reduce_scatter | solution.py:99
  535.7 7.0 %copy.46 = f32[2048,1024]{1,0:T(8,128)} copy(bf16[2048,1024]{0,1:T(8,128)(2,1)} %reduce-scatter.7.cloned.1.call-done) | data formatting | bytes 12582912
  542.7 39.2 %reduce-scatter.5.cloned.1.call-done = bf16[1024,128]{0,1:T(8,128)(2,1)} async-done(((bf16[8192,128]{0,1:T(8,128)(2,1)}), bf16[1024,128]{0,1:T(8,128)(2,1)}) %reduce-scatter.5.cloned.1.call-update) | async-done | bytes 262160 | tf_op jit(solution)/shard_map/reduce_scatter | solution.py:77
  (33 shorter events, 0.3 us)
Async XLA Ops:
  7.2 65.6 %copy-start = (bf16[1024,1024]{1,0:T(8,128)(2,1)S(1)}, bf16[1024,1024]{1,0:T(8,128)(2,1)}, u32[]{:S(2)}) copy-start(bf16[1024,1024]{1,0:T(8,128)(2,1)} %param.11) | copy-start | bytes 6291460
  7.2 33.4 %all-gather.5.cloned.1.call-start = ((), (), s32[]{:S(2)}) async-start(), calls=%async_computation.5 | async-start | bytes 2359296 | tf_op jit(solution)/shard_map/all_gather | solution.py:33
  7.9 62.5 %all-gather.3.cloned.1.call-start = ((), (), s32[]{:S(2)}) async-start(), calls=%async_computation.4 | async-start | bytes 2359296 | tf_op jit(solution)/shard_map/all_gather | solution.py:37
  8.7 154.4 %all-reduce.7.cloned.1.call-start = ((), (), s32[]{:S(2)}) async-start(), calls=%async_computation.10 | async-start | bytes 4194304
  72.8 1.6 copy-start.10
  77.2 2.7 copy-start.4
  77.7 1.0 copy-start.6
  94.6 2.7 copy-start.8
  94.6 2.7 copy-start.11
  101.4 1.2 copy-start.9
  101.5 106.9 %reduce-scatter.11.cloned.1.call-start = ((), (), s32[]{:S(2)}) async-start(), calls=%async_computation.9 | async-start | bytes 2621440 | tf_op jit(solution)/shard_map/reduce_scatter | solution.py:105
  105.3 1.2 copy-start.7
  105.3 148.5 %reduce-scatter.9.cloned.1.call-start = ((), (), s32[]{:S(2)}) async-start(), calls=%async_computation.8 | async-start | bytes 2621440 | tf_op jit(solution)/shard_map/reduce_scatter | solution.py:102
  109.2 1.2 copy-start.5
  109.2 4.2 copy-start.2
  109.2 426.4 %reduce-scatter.7.cloned.1.call-start = ((), (), s32[]{:S(2)}) async-start(), calls=%async_computation.7 | async-start | bytes 20971520 | tf_op jit(solution)/shard_map/reduce_scatter | solution.py:99
  121.7 460.2 %reduce-scatter.5.cloned.1.call-start = ((), (), s32[]{:S(2)}) async-start(), calls=%async_computation.6 | async-start | bytes 2359296 | tf_op jit(solution)/shard_map/reduce_scatter | solution.py:77
  134.5 0.7 copy-start.12
  134.5 1.2 copy-start.3
  535.7 46.2 %copy-start.1 = (bf16[1024,1024]{1,0:T(8,128)(2,1)S(1)}, bf16[1024,1024]{1,0:T(8,128)(2,1)}, u32[]{:S(2)}) copy-start(bf16[1024,1024]{1,0:T(8,128)(2,1)} %param.11) | copy-start | bytes 6291460
Sparse Core Ops, SparseCore 0:
  9.9 30.5 all-gather.4
  42.4 27.8 all-gather.2
  101.6 61.4 all-reduce.6
  165.2 43.0 reduce-scatter.10
  210.5 43.1 reduce-scatter.8
  256.0 279.6 reduce-scatter.6
  539.9 41.9 reduce-scatter.4
where the time goes:
time: 589 us
  waiting for transfers between devices  478 us (81%)
  matrix products  58.7 us (10%)
  local copies, waits for them, and re-layouts  31.3 us (5%)
  between operations  14.4 us (2%)
    reduce_scatter x1, waiting for transfers between devices, body(): lax.psum_scatter(query_part.astype(jnp.bfloat16), 'seq', scatter_dimensio...  280 us
    reduce_scatter x1, waiting for transfers between devices, body(): lax.psum_scatter(key_part.astype(jnp.bfloat16), 'seq', scatter_dimension=...  43.3 us
    reduce_scatter x1, waiting for transfers between devices, body(): lax.psum_scatter(value_part.astype(jnp.bfloat16), 'seq', scatter_dimensio...  40.6 us
    reduce_scatter x1, waiting for transfers between devices, body(): lax.psum_scatter(contract_cols(w_query, query_grad).astype(jnp.bfloat16),...  39.2 us
    all_gather x1, waiting for transfers between devices, body(): whole = lax.all_gather(hidden, 'tensor', axis=2, tiled=True)[0]  28.5 us
    unnamed x8, waiting for transfers between devices  25.7 us
    all_gather x1, waiting for transfers between devices, body(): every = lax.all_gather(neighbours, 'tensor', axis=1, tiled=True)[0]  20.9 us
    unnamed x37, local copies, waits for them, and re-layouts  18.9 us
  transfers between devices with their start and end apart: 7, of which 7 were waited for; matrix products, arithmetic and copies ran while one was open for 10% of the time, Pallas kernels for 0%

commit v1 on v0

--- a/solution.py
+++ b/solution.py
@@ -30,8 +30,10 @@
     span_count = slot_of.shape[1]
     lag = SPAN - 1
     scale = 1.0 / math.sqrt(HS)
-    whole = lax.all_gather(hidden, "tensor", axis=2, tiled=True)[0]
-    length = whole.shape[0]
+    length = hidden.shape[1]
+    first = lag // 16 * 16
+    skip = lag - first
+    whole = lax.all_gather(hidden[0, first:], "tensor", axis=1, tiled=True)
     query = jnp.dot(whole, w_query, preferred_element_type=jnp.float32).astype(jnp.bfloat16)
     slots = slot_of[0].reshape(-1)
     every = lax.all_gather(neighbours, "tensor", axis=1, tiled=True)[0]
@@ -42,7 +44,7 @@
     shaped_keys = keys.reshape(span_count, -1, heads_here, HS)
     shaped_values = values.reshape(span_count, -1, heads_here, HS)
     blank = jnp.zeros((lag, width), jnp.bfloat16)
-    shifted = jnp.concatenate([query[lag:], blank], 0).reshape(span_count, SPAN, heads_here, HS)
+    shifted = jnp.concatenate([query[skip:], blank], 0).reshape(span_count, SPAN, heads_here, HS)
     grads = jnp.concatenate([out_grad[0][lag:], blank], 0).reshape(span_count, SPAN, heads_here, HS)
     scores = (
         jnp.einsum("uqhd,ukhd->uhqk", shifted, shaped_keys, preferred_element_type=jnp.float32)
@@ -73,14 +75,17 @@
         .astype(jnp.bfloat16)
         .reshape(-1, width)
     )
-    query_grad = jnp.concatenate([blank, shift_grad.reshape(length, width)[: length - lag]], 0)
+    query_grad = jnp.concatenate(
+        [blank[:skip], shift_grad.reshape(length, width)[: length - lag]], 0
+    )
     feature_grad = lax.psum_scatter(
-        contract_cols(w_query, query_grad).astype(jnp.bfloat16),
+        contract_cols(query_grad, w_query).astype(jnp.bfloat16),
         "tensor",
-        scatter_dimension=0,
+        scatter_dimension=1,
         tiled=True,
-    ).astype(jnp.float32)
-    hidden_grad = feature_grad.T.astype(jnp.bfloat16)[None]
+    )
+    early = jnp.zeros((first, feature_grad.shape[1]), jnp.bfloat16)
+    hidden_grad = jnp.concatenate([early, feature_grad], 0)[None]
     local_term = contract_cols(key_grad, w_key) + contract_cols(value_grad, w_value)
     flat_bf = local_term.astype(jnp.bfloat16).reshape(slots.shape[0], -1)
     wanted = lax.iota(jnp.int32, slot_count * lax.axis_size("tensor"))
@@ -92,21 +97,14 @@
         tiled=True,
     )
     neighbour_grad = placed.reshape(1, slot_count, R, DE)
-    query_part = contract_rows(whole, query_grad)
-    key_part = contract_rows(states, key_grad)
-    value_part = contract_rows(states, value_grad)
-    summed = (
-        lax.psum_scatter(
-            query_part.astype(jnp.bfloat16), "seq", scatter_dimension=0, tiled=True
-        ).astype(jnp.float32),
-        lax.psum_scatter(
-            key_part.astype(jnp.bfloat16), "seq", scatter_dimension=0, tiled=True
-        ).astype(jnp.float32),
-        lax.psum_scatter(
-            value_part.astype(jnp.bfloat16), "seq", scatter_dimension=0, tiled=True
-        ).astype(jnp.float32),
-    )
-    return (attended, hidden_grad, neighbour_grad, summed[0], summed[1], summed[2])
+    tokens_all = lax.all_to_all(whole, "seq", split_axis=1, concat_axis=0, tiled=True)
+    grads_all = lax.all_gather(query_grad, "seq", axis=0, tiled=True)
+    query_part = contract_rows(tokens_all, grads_all)
+    both = contract_rows(states, jnp.concatenate([key_grad, value_grad], 1))
+    both = lax.psum_scatter(
+        both.astype(jnp.bfloat16), "seq", scatter_dimension=0, tiled=True
+    ).astype(jnp.float32)
+    return (attended, hidden_grad, neighbour_grad, query_part, both[:, :width], both[:, width:])
 
 
 def solution(mesh):

time: 589 us -> 291 us (0.49)
  waiting for transfers between devices: 478 us -> 135 us
  blocking collectives: 0 us -> 40 us
  local copies, waits for them, and re-layouts: 31.3 us -> 40.3 us
    reduce_scatter x4 -> x2, waiting for transfers between devices: 403 us -> 88.6 us  [the longest x1 77.2 us: body(): lax.psum_scatter(both.astype(jnp.bfloat16), 'seq', scatter_dimension=0, t...]
    all_gather x0 -> x1, blocking collectives: none -> 40 us  [body(): grads_all = lax.all_gather(query_grad, 'seq', axis=0, tiled=True)]
    unnamed x8 -> x6, waiting for transfers between devices: 25.7 us -> 0.76 us
    dot_general x3 -> x2, matrix products: 13.5 us -> 10 us  [contract_rows(): lax.dot_general(left, right, (((0,), (0,)), ((), ())), preferred_element_...]
    unnamed x37 -> x43, local copies, waits for them, and re-layouts: 18.9 us -> 19.1 us
  transfers between devices with their start and end apart: 7 -> 6, of which waited for: 7 -> 4; matrix products, arithmetic and copies ran while one was open for 10% -> 19% of each run, Pallas kernels for 0% -> 0%
where the time goes in v1:
time: 291 us; the launch traced here: 290 us
  waiting for transfers between devices  135 us (46%)
  matrix products  55.2 us (19%)
  local copies, waits for them, and re-layouts  40.3 us (14%)
  blocking collectives  40 us (14%)
  between operations  14.1 us (5%)
  starting transfers between devices  4.64 us (2%)
    reduce_scatter x1, waiting for transfers between devices, body(): lax.psum_scatter(both.astype(jnp.bfloat16), 'seq', scatter_dimension=0, t...  77.2 us
    all_gather x1, blocking collectives, body(): grads_all = lax.all_gather(query_grad, 'seq', axis=0, tiled=True)  40 us
    all_gather x1, waiting for transfers between devices, body(): whole = lax.all_gather(hidden[0, first:], 'tensor', axis=1, tiled=True)  24.7 us
    all_gather x1, waiting for transfers between devices, body(): every = lax.all_gather(neighbours, 'tensor', axis=1, tiled=True)[0]  20.5 us
    unnamed x43, local copies, waits for them, and re-layouts  19.1 us
    dot_general x3, matrix products, contract_cols(): lax.dot_general(left, right, (((1,), (1,)), ((), ())), preferred_element_...  16.3 us
    reduce_scatter x1, waiting for transfers between devices, body(): lax.psum_scatter(contract_cols(query_grad, w_query).astype(jnp.bfloat16),...  11.4 us
    dot_general x2, matrix products, contract_rows(): lax.dot_general(left, right, (((0,), (0,)), ((), ())), preferred_element_...  10 us
  transfers between devices with their start and end apart: 6, of which 4 were waited for; matrix products, arithmetic and copies ran while one was open for 19% of the time, Pallas kernels for 0%

profile of v1, /device:TPU:0, one launch (start us, length us, event | category | flops | bytes accessed | tf_op | source)
XLA Modules:
  0.0 290.2 jit_solution(1673916131008584119)
XLA Ops:
  7.2 0.0 copy-start
  7.2 0.0 all-gather.6.cloned.1.call-start
  7.2 1.7 slice.25
  9.0 0.0 all-gather.6.cloned.1.call-update
  9.0 0.0 all-gather.4.cloned.1.call-start
  9.0 0.7 all-gather.4.cloned.1.call-update
  9.7 0.0 all-reduce.8.cloned.1.call-start
  9.8 0.8 reshape_squeeze.5
  10.6 0.8 reshape_squeeze.6
  11.3 0.9 slice_bitcast_fusion
  12.3 0.8 copy.66
  13.1 0.1 broadcast_bitcast_fusion
  13.1 24.7 %all-gather.6.cloned.1.call-done = bf16[1,80,8192]{2,1,0:T(8,128)(2,1)} async-done(((bf16[1,80,1024]{2,1,0:T(8,128)(2,1)}), bf16[1,80,8192]{2,1,0:T(8,128)(2,1)}) %all-gather.6.cloned.1.call-update) | async-done | bytes 1310736 | tf_op jit(solution)/shard_map/all_gather | solution.py:36
  37.8 9.2 %fusion.12 = bf16[80,1024]{1,0:T(8,128)(2,1)S(1)} fusion(bf16[8192,1024]{1,0:T(8,128)(2,1)} %param.10, bf16[1,80,8192]{2,1,0:T(8,128)(2,1)} %all-gather.6.cloned.1.call-done), kind=kOutput, calls=%fused_computation.23 | convolution fusion | flops 1342177280 | bytes 18251776 | tf_op jit(solution)/shard_map/dot_general | solution.py:37
  47.2 20.5 %all-gather.4.cloned.1.call-done = bf16[1,8,128,1024]{3,2,0,1:T(8,128)(2,1)} async-done(((bf16[1,1,128,1024]{3,2,0,1:T(8,128)(2,1)}), bf16[1,8,128,1024]{3,2,0,1:T(8,128)(2,1)}) %all-gather.4.cloned.1.call-update) | async-done | bytes 2097168 | tf_op jit(solution)/shard_map/all_gather | solution.py:39
  67.6 2.2 gather_fusion
  69.9 0.2 bitcast_select_fusion
  70.1 1.3 fusion.5
  71.4 0.3 copy.63
  71.6 0.5 fusion.11
  72.2 1.0 copy-done.10
  73.1 1.2 fusion.27
  74.3 3.2 %fusion.7 = bf16[2,256,8,128]{1,3,2,0:T(8,128)(2,1)} fusion(bf16[2,64,8,128]{3,2,1,0:T(8,128)(2,1)} %bitcast.93, f32[2,8,64,256]{3,2,1,0:T(8,128)} %copy-done.10), kind=kOutput, calls=%fused_computation.17 | convolution fusion | flops 68158720 | bytes 2359296 | tf_op jit(solution)/shard_map/uhqk,uqhd->ukhd/dot_general | solution.py:74
  77.6 3.2 %fusion.4 = bf16[64,8,8,128]{3,1,2,0:T(8,128)(2,1)S(1)} fusion(bf16[512,1024]{1,0:T(8,128)(2,1)} %copy-done.7, bf16[1024,1024]{1,0:T(8,128)(2,1)} %param.12), kind=kOutput, calls=%fused_computation.14 | convolution fusion | flops 1074266112 | bytes 4194304 | tf_op jit(solution)/shard_map/dot_general | solution.py:43
  80.7 0.0 copy-start.9
  80.7 0.3 copy.64
  81.0 1.0 copy-done.3
  82.0 1.5 fusion.21
  83.5 3.3 %fusion.16 = bf16[2,64,8,128]{3,1,2,0:T(8,128)(2,1)} fusion(f32[2,8,64,256]{3,2,1,0:T(8,128)} %fusion.27, f32[2,8,64,256]{3,2,1,0:T(8,128)} %fusion.21, bf16[2,256,8,128]{3,2,1,0:T(8,128)(2,1)S(1)} %bitcast.86), kind=kOutput, calls=%fused_computation.29 | convolution fusion | flops 68551936 | bytes 3407872 | tf_op jit(solution)/shard_map/uhqk,ukhd->uqhd/dot_general | solution.py:65
  86.8 2.8 fusion.6
  89.6 2.6 copy.59
  92.2 1.5 copy.57
  93.7 0.2 copy.55
  93.9 2.7 fusion.46
  96.6 1.3 add_convert_fusion
  97.9 0.8 reshape.94
  98.7 2.0 convolution_convert_fusion
  100.7 0.0 all-reduce.8.cloned.1.call-update
  100.8 0.0 reduce-scatter.3.cloned.1.call-start
  100.8 12.4 %convolution_convert_fusion.1 = bf16[80,8192]{1,0:T(8,128)(2,1)} fusion(bf16[8192,1024]{1,0:T(8,128)(2,1)} %param.10, bf16[65,1024]{1,0:T(8,128)(2,1)S(1)} %slice.37), kind=kOutput, calls=%fused_computation.3 | convolution fusion | flops 1342832640 | bytes 18221056 | tf_op jit(solution)/shard_map/dot_general | solution.py:21
  113.2 0.0 reduce-scatter.3.cloned.1.call-update
  113.2 0.0 reduce-scatter.5.cloned.1.call-start
  113.3 0.5 copy_bitcast_fusion
  113.8 0.6 copy-done.8
  114.5 4.4 %convolution_convert_fusion.2 = bf16[1024,2048]{1,0:T(8,128)(2,1)} fusion(bf16[512,1024]{1,0:T(8,128)(2,1)S(1)} %copy-done.8, bf16[512,1024]{1,0:T(8,128)(2,1)S(1)} %get-tuple-element.32, bf16[512,1024]{1,0:T(8,128)(2,1)S(1)} %get-tuple-element.33), kind=kOutput, calls=%fused_computation.5 | convolution fusion | flops 2153775104 | bytes 7340032 | tf_op jit(solution)/shard_map/dot_general | solution.py:15
  118.8 0.0 reduce-scatter.5.cloned.1.call-update
  118.9 1.3 copy-done.2
  120.2 1.0 all_to_all.14
  121.2 0.0 copy-start.15
  121.2 1.8 copy.60
  123.0 4.4 %all-to-all-start = ((bf16[80,4,2048]{2,0,1:T(8,128)(2,1)}), bf16[80,4,2048]{2,0,1:T(8,128)(2,1)S(1)}, u32[]{:S(2)}, u32[]{:S(2)}) async-start(bf16[80,4,2048]{2,0,1:T(8,128)(2,1)} %copy.60), calls=%async_computation.1 | async-start | bytes 2621440 | tf_op jit(solution)/shard_map/all_to_all | solution.py:100
  127.4 0.6 dynamic-slice
  128.0 2.0 fusion.15
  130.0 0.2 copy.51
  130.3 0.7 pad_bitcast_fusion.2
  131.0 40.0 %all_gather.11 = bf16[320,1024]{1,0:T(8,128)(2,1)S(1)} all-gather(bf16[80,1024]{1,0:T(8,128)(2,1)S(1)} %concatenate.21), channel_id=1, replica_groups=mesh['seq'=4,'tensor'=8] {'seq'}, dimensions={0}, use_global_device_ids=true | all-gather | bytes 819200 | tf_op jit(solution)/shard_map/all_gather | solution.py:101
  171.0 5.6 %convolution_bitcast_fusion = f32[2048,1024]{0,1:T(8,128)} fusion(bf16[320,1024]{1,0:T(8,128)(2,1)S(1)} %all_gather.11, bf16[320,2048]{1,0:T(8,128)(2,1)S(1)} %bitcast.82), kind=kOutput, calls=%fused_computation.4 | convolution fusion | flops 1342177280 | bytes 10354688 | tf_op jit(solution)/shard_map/dot_general | solution.py:15
  176.6 9.3 %copy.61 = f32[2048,1024]{1,0:T(8,128)} copy(f32[2048,1024]{0,1:T(8,128)} %convolution_bitcast_fusion) | data formatting | bytes 16777216
  185.9 3.8 %dynamic-slice_reduce_fusion = bf16[131072]{0:T(1024)(128)(2,1)S(1)} fusion(bf16[8,131072]{1,0:T(8,128)(2,1)} %all-reduce.8.cloned.1.call-done, u32[]{:T(128)} %bitcast.16), kind=kLoop, calls=%fused_computation.41 | loop fusion | bytes 524292
  189.7 0.8 reshape.95
  190.6 11.4 %reduce-scatter.3.cloned.1.call-done = bf16[80,1024]{1,0:T(8,128)(2,1)} async-done(((bf16[80,8192]{1,0:T(8,128)(2,1)}), bf16[80,1024]{1,0:T(8,128)(2,1)}) %reduce-scatter.3.cloned.1.call-update) | async-done | bytes 163856 | tf_op jit(solution)/shard_map/reduce_scatter | solution.py:81
  202.0 1.8 pad_bitcast_fusion
  203.8 77.2 %reduce-scatter.5.cloned.1.call-done = bf16[256,2048]{1,0:T(8,128)(2,1)} async-done(((bf16[1024,2048]{1,0:T(8,128)(2,1)}), bf16[256,2048]{1,0:T(8,128)(2,1)}) %reduce-scatter.5.cloned.1.call-update) | async-done | bytes 1048592 | tf_op jit(solution)/shard_map/reduce_scatter | solution.py:104
  280.9 2.8 fusion.47
  (39 shorter events, 0.4 us)
Async XLA Ops:
  7.2 62.9 %copy-start = (bf16[1024,1024]{1,0:T(8,128)(2,1)S(1)}, bf16[1024,1024]{1,0:T(8,128)(2,1)}, u32[]{:S(2)}) copy-start(bf16[1024,1024]{1,0:T(8,128)(2,1)} %param.11) | copy-start | bytes 6291460
  7.2 30.6 %all-gather.6.cloned.1.call-start = ((), (), s32[]{:S(2)}) async-start(), calls=%async_computation.6 | async-start | bytes 1474560 | tf_op jit(solution)/shard_map/all_gather | solution.py:36
  9.0 58.7 %all-gather.4.cloned.1.call-start = ((), (), s32[]{:S(2)}) async-start(), calls=%async_computation.3 | async-start | bytes 2359296 | tf_op jit(solution)/shard_map/all_gather | solution.py:39
  9.7 176.1 %all-reduce.8.cloned.1.call-start = ((), (), s32[]{:S(2)}) async-start(), calls=%async_computation.7 | async-start | bytes 4194304
  10.5 36.5 %copy-start.12 = (s32[4]{0:T(128)}, s32[4]{0:T(128)S(1)}, u32[]{:S(2)}) copy-start(s32[4]{0:T(128)S(1)} %reshape_squeeze.5) | copy-start | bytes 52
  70.1 1.3 copy-start.7
  72.2 1.0 copy-start.10
  80.7 1.3 copy-start.9
  81.0 1.0 copy-start.3
  89.6 4.1 %copy-start.11 = (bf16[2,64,8,128]{3,1,2,0:T(8,128)(2,1)S(1)}, bf16[2,64,8,128]{3,1,2,0:T(8,128)(2,1)}, u32[]{:S(2)}) copy-start(bf16[2,64,8,128]{3,1,2,0:T(8,128)(2,1)} %fusion.16) | copy-start | bytes 786436
  93.9 2.7 copy-start.5
  93.9 2.7 copy-start.14
  97.9 0.8 copy-start.13
  100.8 12.5 %copy-start.6 = (bf16[2,256,8,128]{3,2,1,0:T(8,128)(2,1)S(1)}, bf16[2,256,8,128]{3,2,1,0:T(8,128)(2,1)}, u32[]{:S(2)}) copy-start(bf16[2,256,8,128]{3,2,1,0:T(8,128)(2,1)} %copy.57) | copy-start | bytes 3145732
  100.8 101.2 %reduce-scatter.3.cloned.1.call-start = ((), (), s32[]{:S(2)}) async-start(), calls=%async_computation.4 | async-start | bytes 1474560 | tf_op jit(solution)/shard_map/reduce_scatter | solution.py:81
  113.2 1.2 copy-start.8
  113.2 167.7 %reduce-scatter.5.cloned.1.call-start = ((), (), s32[]{:S(2)}) async-start(), calls=%async_computation.5 | async-start | bytes 5242880 | tf_op jit(solution)/shard_map/reduce_scatter | solution.py:104
  118.8 1.3 copy-start.2
  121.2 6.2 %copy-start.15 = (u32[32]{0:T(128)S(1)}, u32[32]{0:T(128)}, u32[]{:S(2)}) copy-start(u32[32]{0:T(128)} %constant.40) | copy-start | bytes 388
  123.0 5.0 %copy-start.4 = (bf16[64,8,8,128]{3,2,1,0:T(8,128)(2,1)S(1)}, bf16[64,8,8,128]{3,2,1,0:T(8,128)(2,1)}, u32[]{:S(2)}) copy-start(bf16[64,8,8,128]{3,2,1,0:T(8,128)(2,1)} %copy-done.3) | copy-start | bytes 3145732
  123.0 48.0 %all-to-all-start = ((bf16[80,4,2048]{2,0,1:T(8,128)(2,1)}), bf16[80,4,2048]{2,0,1:T(8,128)(2,1)S(1)}, u32[]{:S(2)}, u32[]{:S(2)}) async-start(bf16[80,4,2048]{2,0,1:T(8,128)(2,1)} %copy.60), calls=%async_computation.1 | async-start | bytes 2621440 | tf_op jit(solution)/shard_map/all_to_all | solution.py:100
  202.0 81.7 %copy-start.1 = (bf16[1024,1024]{1,0:T(8,128)(2,1)S(1)}, bf16[1024,1024]{1,0:T(8,128)(2,1)}, u32[]{:S(2)}) copy-start(bf16[1024,1024]{1,0:T(8,128)(2,1)} %param.11) | copy-start | bytes 6291460
Sparse Core Ops, SparseCore 0:
  10.5 27.2 all-gather.5
  39.7 27.8 all-gather.3
  100.9 61.3 all-reduce.7
  165.4 36.5 reduce-scatter.2
  204.1 76.7 reduce-scatter.4

commit v2 on v1

v2 whole, which is shorter than its diff:
```python
import functools
import math

import jax
import jax.numpy as jnp
from jax import lax
from jax.experimental import pallas as pl
from jax.experimental.pallas import tpu as pltpu
from jax.sharding import PartitionSpec as P

HS = 128
DE = 1024
SPAN = 64
R = 128
TAIL = 16
MESH = pl.DeviceIdType.MESH
BF = jnp.bfloat16
F32 = jnp.float32
VMEM = pl.BlockSpec(memory_space=pltpu.VMEM)
ANY = pl.BlockSpec(memory_space=pl.ANY)
LIMIT = 50 * 2**20


def contract_rows(left, right):
    return lax.dot_general(left, right, (((0,), (0,)), ((), ())), preferred_element_type=F32)


def contract_cols(left, right):
    return lax.dot_general(left, right, (((1,), (1,)), ((), ())), preferred_element_type=F32)


def remote(src, dst, send, recv, axis, index):
    return pltpu.make_async_remote_copy(
        src_ref=src, dst_ref=dst, send_sem=send, recv_sem=recv,
        device_id={axis: index}, device_id_type=MESH,
    )


def gather_kernel(
    n, seqs, hid, nb, og, w_hbm, whole, every, qall, ogall,
    w, acc, w_sem, h_send, h_recv, n_send, n_recv, z_send, z_recv,
):
    me = lax.axis_index("tensor")
    row = lax.axis_index("seq")
    chips = n // 2
    core = lax.rem(me, 2)
    chip = me // 2
    twin = me + 1 - 2 * core
    depth = hid.shape[1]

    def peer(k):
        return lax.rem(chip + k, chips) * 2 + core

    def over(k):
        return lax.rem(row + k, seqs)

    fetch = pltpu.make_async_copy(w_hbm, w, w_sem)
    fetch.start()
    barrier = pltpu.get_barrier_semaphore()
    pl.semaphore_signal(barrier, inc=1, device_id={"tensor": twin}, device_id_type=MESH)

    @pl.loop(1, chips)
    def _(k):
        pl.semaphore_signal(barrier, inc=1, device_id={"tensor": peer(k)}, device_id_type=MESH)

    for k in range(1, seqs):
        pl.semaphore_signal(barrier, inc=1, device_id={"seq": over(k)}, device_id_type=MESH)
    pl.semaphore_wait(barrier, chips + seqs - 1)

    def own(ref, out, send, recv, k, target):
        return remote(ref, out.at[me], send.at[k], recv.at[me], "tensor", target)

    def onward(out, send, recv, k):
        return remote(
            out.at[peer(k)], out.at[peer(k)], send.at[chips + k], recv.at[peer(k)], "tensor", twin
        )

    def arrival(out, send, recv, index):
        return remote(out.at[index], out.at[index], send.at[0], recv.at[index], "tensor", twin)

    def z_copy(ref, out, lane, k):
        return remote(ref, out.at[row], z_send.at[lane, k], z_recv.at[lane, row], "seq", over(k))

    @pl.loop(1, chips)
    def _(k):
        own(hid, whole, h_send, h_recv, k, peer(k)).start()

    own(hid, whole, h_send, h_recv, 0, twin).start()

    @pl.loop(1, chips)
    def _(k):
        own(nb, every, n_send, n_recv, k, peer(k)).start()

    own(nb, every, n_send, n_recv, 0, twin).start()
    for k in range(1, seqs):
        z_copy(og, ogall, 0, k).start()
    whole[me] = hid[...]
    every[me] = nb[...]
    ogall[row] = og[...]
    fetch.wait()

    def add(index):
        part = w[pl.ds(pl.multiple_of(index * depth, depth), depth), :]
        acc[...] += jnp.dot(whole[index], part, preferred_element_type=F32)

    acc[...] = jnp.zeros_like(acc)
    add(me)

    @pl.loop(1, chips)
    def _(k):
        arrival(whole, h_send, h_recv, peer(k)).wait_recv()
        onward(whole, h_send, h_recv, k).start()
        add(peer(k))

    @pl.loop(0, chips)
    def _(k):
        index = peer(k) + 1 - 2 * core
        arrival(whole, h_send, h_recv, index).wait_recv()
        add(index)

    qall[row] = acc[...].astype(BF)
    for k in range(1, seqs):
        z_copy(qall.at[row], qall, 1, k).start()

    @pl.loop(1, chips)
    def _(k):
        arrival(every, n_send, n_recv, peer(k)).wait_recv()
        onward(every, n_send, n_recv, k).start()

    @pl.loop(0, chips)
    def _(k):
        arrival(every, n_send, n_recv, peer(k) + 1 - 2 * core).wait_recv()

    for k in range(1, seqs):
        came = over(k)
        for lane, out in ((0, ogall), (1, qall)):
            remote(
                out.at[came], out.at[came], z_send.at[lane, 0], z_recv.at[lane, came], "seq", came
            ).wait_recv()
            z_copy(og if lane == 0 else qall.at[row], out, lane, k).wait_send()
    for ref, out, send, recv in ((hid, whole, h_send, h_recv), (nb, every, n_send, n_recv)):
        own(ref, out, send, recv, 0, twin).wait_send()

        @pl.loop(1, chips)
        def _(k):
            own(ref, out, send, recv, k, peer(k)).wait_send()
            onward(out, send, recv, k).wait_send()


def gather(n, seqs, hid, nb, og, w_query):
    rows, depth = hid.shape
    width = w_query.shape[1]
    dma = pltpu.SemaphoreType.DMA
    return pl.pallas_call(
        functools.partial(gather_kernel, n, seqs),
        out_shape=(
            jax.ShapeDtypeStruct((n, rows, depth), BF),
            jax.ShapeDtypeStruct((n,) + nb.shape, BF),
            jax.ShapeDtypeStruct((seqs, rows, width), BF),
            jax.ShapeDtypeStruct((seqs, rows, width), BF),
        ),
        in_specs=[VMEM, VMEM, VMEM, ANY],
        out_specs=(VMEM,) * 4,
        scratch_shapes=[
            pltpu.VMEM(w_query.shape, BF),
            pltpu.VMEM((rows, width), F32),
            dma, dma((n,)), dma((n,)), dma((n,)), dma((n,)), dma((2, seqs)), dma((2, seqs)),
        ],
        compiler_params=pltpu.CompilerParams(
            collective_id=0, has_side_effects=True, vmem_limit_bytes=LIMIT
        ),
        name="gather",
    )(hid, nb, og, w_query)


def attention_kernel(spans, q, og, key, value, mixed, qg, kg, vg, sgsh):
    scale = 1.0 / math.sqrt(HS)
    reach = key.shape[0] // spans
    for u in range(spans):
        here = pl.ds(u * SPAN, SPAN if u < spans - 1 else TAIL)
        rows = pl.ds(u * reach, reach)
        qu, gu, ku, vu = q[here, :], og[here, :], key[rows, :], value[rows, :]
        raised = jnp.exp(contract_cols(qu, ku) * scale)
        shares = raised / jnp.sum(raised, axis=-1, keepdims=True)
        share_bf = shares.astype(BF)
        mixed[here, :] = jnp.dot(share_bf, vu, preferred_element_type=F32).astype(BF)
        share_grad = contract_cols(gu, vu)
        centre = jnp.sum(shares * share_grad, axis=-1, keepdims=True)
        score_grad = (shares * (share_grad - centre) * scale).astype(BF)
        qg[here, :] = jnp.dot(score_grad, ku, preferred_element_type=F32).astype(BF)
        kg[rows, :] = contract_rows(score_grad, qu).astype(BF)
        vg[rows, :] = contract_rows(share_bf, gu).astype(BF)
        sgsh[0, 0, here, :] = score_grad
        sgsh[1, 0, here, :] = share_bf


def attention(spans, q, og, keys, values):
    rows, width = q.shape
    heads = width // HS
    many = keys.shape[0]
    narrow = pl.BlockSpec((rows, HS), lambda h: (0, h))
    tall = pl.BlockSpec((many, HS), lambda h: (0, h))
    reach = many // spans
    return pl.pallas_call(
        functools.partial(attention_kernel, spans),
        grid=(heads,),
        out_shape=(
            jax.ShapeDtypeStruct((rows, width), BF),
            jax.ShapeDtypeStruct((rows, width), BF),
            jax.ShapeDtypeStruct((many, width), BF),
            jax.ShapeDtypeStruct((many, width), BF),
            jax.ShapeDtypeStruct((2, heads, rows, reach), BF),
        ),
        in_specs=[narrow, narrow, tall, tall],
        out_specs=(
            narrow, narrow, tall, tall,
            pl.BlockSpec((2, 1, rows, reach), lambda h: (0, h, 0, 0)),
        ),
        compiler_params=pltpu.CompilerParams(vmem_limit_bytes=LIMIT),
        name="attention",
    )(q, og, keys, values)


def exchange_kernel(
    n, seqs, hs, ns, sgsh, qg, hid, nbr, zall, qgall,
    h_in, n_in, h_send, h_recv, n_send, n_recv, z_send, z_recv,
):
    me = lax.axis_index("tensor")
    row = lax.axis_index("seq")

    def peer(k):
        return lax.rem(me + k, n)

    barrier = pltpu.get_barrier_semaphore()

    @pl.loop(1, n)
    def _(k):
        pl.semaphore_signal(barrier, inc=1, device_id={"tensor": peer(k)}, device_id_type=MESH)

    for k in range(1, seqs):
        pl.semaphore_signal(
            barrier, inc=1, device_id={"seq": lax.rem(row + k, seqs)}, device_id_type=MESH
        )
    pl.semaphore_wait(barrier, n - 1 + seqs - 1)

    def scatter(ref, into, send, recv, k):
        return remote(ref.at[peer(k)], into.at[me], send.at[k], recv.at[me], "tensor", peer(k))

    outs = (qgall, zall)
    owns = (qg, sgsh)

    def hop(side, h, lane):
        step = 1 - 2 * side
        origin = row - step * h
        src = owns[lane] if h == 0 else outs[lane].at[origin]
        return remote(
            src, outs[lane].at[origin], z_send.at[side, h, lane], z_recv.at[side, h, lane],
            "seq", row + step,
        )

    def sends(side, h):
        if side == 0:
            return (row - h >= 0) & (row + 1 < seqs)
        return (row + h < seqs) & (row >= 1)

    def arrives(side, h):
        return row - 1 - h >= 0 if side == 0 else row + 1 + h < seqs

    def arrived(side, h, lane):
        step = 1 - 2 * side
        origin = row - step * (h + 1)
        return remote(
            outs[lane].at[origin], outs[lane].at[origin],
            z_send.at[side, h, lane], z_recv.at[side, h, lane], "seq", row - step,
        )

    for side in range(2):
        @pl.when(sends(side, 0))
        def _():
            for lane in range(2):
                hop(side, 0, lane).start()

    @pl.loop(1, n)
    def _(k):
        scatter(hs, h_in, h_send, h_recv, k).start()
        scatter(ns, n_in, n_send, n_recv, k).start()

    for lane in range(2):
        outs[lane][row] = owns[lane][...]
    for h in range(seqs - 1):
        for lane in range(2):
            for side in range(2):
                @pl.when(arrives(side, h))
                def _():
                    arrived(side, h, lane).wait_recv()

                if h + 1 < seqs - 1:
                    @pl.when(sends(side, h + 1))
                    def _():
                        hop(side, h + 1, lane).start()

        if h == 0:
            for ref, into, send, recv, out in (
                (hs, h_in, h_send, h_recv, hid), (ns, n_in, n_send, n_recv, nbr)
            ):
                @pl.loop(1, n)
                def _(k):
                    remote(
                        into.at[peer(k)], into.at[peer(k)], send.at[0], recv.at[peer(k)],
                        "tensor", peer(k),
                    ).wait_recv()

                into[me] = ref[me]
                total = into[0].astype(F32)
                for j in range(1, n):
                    total = total + into[j].astype(F32)
                out[...] = total.astype(BF)

    for side in range(2):
        for h in range(seqs - 1):
            @pl.when(sends(side, h))
            def _():
                for lane in range(2):
                    hop(side, h, lane).wait_send()

    @pl.loop(1, n)
    def _(k):
        scatter(hs, h_in, h_send, h_recv, k).wait_send()
        scatter(ns, n_in, n_send, n_recv, k).wait_send()


def exchange(n, seqs, hs, ns, sgsh, qg):
    dma = pltpu.SemaphoreType.DMA
    return pl.pallas_call(
        functools.partial(exchange_kernel, n, seqs),
        out_shape=(
            jax.ShapeDtypeStruct(hs.shape[1:], BF),
            jax.ShapeDtypeStruct(ns.shape[1:], BF),
            jax.ShapeDtypeStruct((seqs,) + sgsh.shape, BF),
            jax.ShapeDtypeStruct((seqs,) + qg.shape, BF),
        ),
        in_specs=[VMEM] * 4,
        out_specs=(VMEM,) * 4,
        scratch_shapes=[
            pltpu.VMEM(hs.shape, BF), pltpu.VMEM(ns.shape, BF),
            dma((n,)), dma((n,)), dma((n,)), dma((n,)),
            dma((2, seqs - 1, 2)), dma((2, seqs - 1, 2)),
        ],
        compiler_params=pltpu.CompilerParams(
            collective_id=1, has_side_effects=True, vmem_limit_bytes=LIMIT
        ),
        name="exchange",
    )(hs, ns, sgsh, qg)


def weight_kernel(spans, seqs, sgsh, q, og, picks, wk, wv):
    reach = sgsh.shape[-1]
    for lane, right, out in ((0, q, wk), (1, og, wv)):
        total = jnp.zeros(out.shape, F32)
        for s in range(seqs):
            for u in range(spans):
                here = pl.ds(u * SPAN, SPAN if u < spans - 1 else TAIL)
                grad = contract_rows(sgsh[s, lane, 0, here, :], right[s, here, :]).astype(BF)
                total += contract_rows(picks[s, pl.ds(u * reach, reach), :], grad)
        out[...] = total


def weights(spans, sgsh, q, og, picks):
    seqs, _, heads, rows, reach = sgsh.shape
    cols = picks.shape[2]
    narrow = pl.BlockSpec((seqs, rows, HS), lambda h: (0, 0, h))
    result = jax.ShapeDtypeStruct((cols, heads * HS), F32)
    return pl.pallas_call(
        functools.partial(weight_kernel, spans, seqs),
        grid=(heads,),
        out_shape=(result, result),
        in_specs=[
            pl.BlockSpec((seqs, 2, 1, rows, reach), lambda h: (0, 0, h, 0, 0)),
            narrow, narrow,
            pl.BlockSpec(picks.shape, lambda h: (0, 0, 0)),
        ],
        out_specs=(pl.BlockSpec((cols, HS), lambda h: (0, h)),) * 2,
        compiler_params=pltpu.CompilerParams(vmem_limit_bytes=LIMIT),
        name="weights",
    )(sgsh, q, og, picks)


def body(n, seqs, hidden, neighbours, slot_of, w_query, w_key, w_value, out_grad):
    width = w_query.shape[1]
    length = hidden.shape[1]
    slot_count = neighbours.shape[1]
    spans = slot_of.shape[1]
    lag = SPAN - 1
    rows = (spans - 1) * SPAN + TAIL
    slots = slot_of[0].reshape(-1)

    def later(x):
        return jnp.pad(x[lag:], ((0, rows - (length - lag)), (0, 0)))

    def back(x):
        return jnp.pad(x[: length - lag], ((lag, 0), (0, 0)))[None]

    og = later(out_grad[0])
    row = lax.axis_index("seq")
    whole, every, qall, ogall = gather(
        n, seqs, later(hidden[0]), neighbours[0].reshape(slot_count * R, DE), og, w_query
    )
    states = jnp.take(every.reshape(-1, R, DE), slots, axis=0).reshape(-1, DE)
    tokens_all = lax.all_to_all(
        whole.reshape((seqs, n // seqs) + whole.shape[1:]), "seq", 0, 0, tiled=True
    )
    picks = lax.all_to_all(
        states.reshape(-1, seqs, DE // seqs).transpose(1, 0, 2), "seq", 0, 0, tiled=True
    )
    keys = jnp.dot(states, w_key, preferred_element_type=F32).astype(BF)
    values = jnp.dot(states, w_value, preferred_element_type=F32).astype(BF)
    query = lax.dynamic_index_in_dim(qall, row, 0, keepdims=False)
    mixed, qg, kg, vg, sgsh = attention(spans, query, og, keys, values)
    feature_terms = lax.dot_general(
        w_query.reshape(n, -1, width), qg, (((2,), (1,)), ((), ())), preferred_element_type=F32
    ).astype(BF)
    feature_terms = feature_terms.transpose(0, 2, 1)
    terms = (contract_cols(kg, w_key) + contract_cols(vg, w_value)).astype(BF)
    terms = jnp.concatenate([terms.reshape(-1, R, DE), jnp.zeros((1, R, DE), BF)], 0)
    wanted = lax.iota(jnp.int32, slot_count * n)[:, None] == slots[None, :]
    place = jnp.where(wanted.any(1), jnp.argmax(wanted, 1).astype(jnp.int32), slots.shape[0])
    placed = jnp.take(terms, place, axis=0).reshape(n, slot_count * R, DE)
    hid, nbr, zall, qgall = exchange(n, seqs, feature_terms, placed, sgsh, qg)
    query_part = lax.dot_general(
        tokens_all.transpose(1, 3, 0, 2).reshape(-1, seqs * rows),
        qgall.reshape(seqs * rows, width),
        (((1,), (0,)), ((), ())),
        preferred_element_type=F32,
    )
    wk, wv = weights(spans, zall, qall, ogall, picks)
    return (
        back(mixed), back(hid), nbr.reshape(1, slot_count, R, DE), query_part, wk, wv
    )


def solution(mesh):
    return jax.shard_map(
        functools.partial(body, mesh.shape["tensor"], mesh.shape["seq"]),
        mesh=mesh,
        in_specs=(
            P("seq", None, "tensor"),
            P("seq", "tensor", None, None),
            P("seq", None, None),
            P(None, "tensor"),
            P(None, "tensor"),
            P(None, "tensor"),
            P("seq", None, "tensor"),
        ),
        out_specs=(
            P("seq", None, "tensor"),
            P("seq", None, "tensor"),
            P("seq", "tensor", None, None),
            P("seq", "tensor"),
            P("seq", "tensor"),
            P("seq", "tensor"),
        ),
        check_vma=False,
    )
```

time: 291 us -> 202 us (0.69)
  waiting for transfers between devices: 135 us -> 0.01 us
  Pallas kernels: 0 us -> 124 us
  blocking collectives: 40 us -> 0 us
  matrix products: 55.2 us -> 26.4 us
  between operations: 14.1 us -> 0.9 us
  local copies, waits for them, and re-layouts: 40.3 us -> 28.6 us
  other arithmetic: 1.41 us -> 8.65 us
  starting transfers between devices: 4.64 us -> 10.3 us
    pallas_call x0 -> x4, Pallas kernels: none -> 124 us  [the longest x1 61.2 us: exchange(): pl.pallas_call(functools.partial(exchange_kernel, n, seqs), out_shape=(ja...]
    reduce_scatter x2 -> x0, waiting for transfers between devices: 88.6 us -> none  [the longest x1 77.2 us: body(): lax.psum_scatter(both.astype(jnp.bfloat16), 'seq', scatter_dimension=0, t...]
    all_gather x2 -> x0, waiting for transfers between devices: 45.2 us -> none  [the longest x1 24.7 us: body(): whole = lax.all_gather(hidden[0, first:], 'tensor', axis=1, tiled=True)]
    all_gather x1 -> x0, blocking collectives: 40 us -> none  [body(): grads_all = lax.all_gather(query_grad, 'seq', axis=0, tiled=True)]
    dot_general x12 -> x4, matrix products: 38.9 us -> 22.8 us  [the longest x1 11 us: body(): lax.dot_general(w_query.reshape(n, -1, width), qg, (((2,), (1,)), ((), ()...]
    dot_general x3 -> x2, matrix products: 16.3 us -> 3.54 us  [contract_cols(): lax.dot_general(left, right, (((1,), (1,)), ((), ())), preferred_element_...]
    unnamed x43 -> x46, local copies, waits for them, and re-layouts: 19.1 us -> 9.65 us
    all_to_all x1 -> x2, starting transfers between devices: 4.44 us -> 10.3 us  [the longest x1 5.25 us: body(): lax.all_to_all(states.reshape(-1, seqs, DE // seqs).transpose(1, 0, 2), '...]
  transfers between devices with their start and end apart: 6 -> 2, of which waited for: 4 -> 0; matrix products, arithmetic and copies ran while one was open for 19% -> 19% of each run, Pallas kernels for 0% -> 45%
where the time goes in v2:
time: 202 us; the launch traced here: 199 us
  Pallas kernels  124 us (61%)
  local copies, waits for them, and re-layouts  28.6 us (14%)
  matrix products  26.4 us (13%)
  starting transfers between devices  10.3 us (5%)
  other arithmetic  8.65 us (4%)
    pallas_call x1, Pallas kernels, exchange(): pl.pallas_call(functools.partial(exchange_kernel, n, seqs), out_shape=(ja...  61.2 us
    pallas_call x1, Pallas kernels, gather(): pl.pallas_call(functools.partial(gather_kernel, n, seqs), out_shape=(jax....  34.3 us
    pallas_call x1, Pallas kernels, weights(): pl.pallas_call(functools.partial(weight_kernel, spans, seqs), grid=(heads...  18.5 us
    dot_general x1, matrix products, body(): lax.dot_general(w_query.reshape(n, -1, width), qg, (((2,), (1,)), ((), ()...  11 us
    pallas_call x1, Pallas kernels, attention(): pl.pallas_call(functools.partial(attention_kernel, spans), grid=(heads,),...  10.5 us
    unnamed x46, local copies, waits for them, and re-layouts  9.65 us
    dot_general x1, matrix products, body(): lax.dot_general(tokens_all.transpose(1, 3, 0, 2).reshape(-1, seqs * rows)...  5.78 us
    all_to_all x1, starting transfers between devices, body(): lax.all_to_all(states.reshape(-1, seqs, DE // seqs).transpose(1, 0, 2), '...  5.25 us
  transfers between devices with their start and end apart: 2, of which 0 were waited for; matrix products, arithmetic and copies ran while one was open for 19% of the time, Pallas kernels for 45%

profile of v2, /device:TPU:0, one launch (start us, length us, event | category | flops | bytes accessed | tf_op | source)
XLA Modules:
  0.0 199.4 jit_solution(16641399306576507994)
XLA Ops:
  0.6 0.0 copy-start
  0.6 0.9 reshape_squeeze.10
  1.6 0.8 reshape_squeeze.9
  2.3 0.9 slice_bitcast_fusion
  3.3 0.9 slice_bitcast_fusion.1
  4.3 0.1 broadcast_bitcast_fusion
  4.4 0.9 copy-done.14
  5.3 34.3 %gather.21 = (bf16[8,80,1024]{2,1,0:T(8,128)(2,1)S(1)}, bf16[8,128,1024]{2,1,0:T(8,128)(2,1)}, bf16[4,80,1024]{2,1,0:T(8,128)(2,1)S(1)}, bf16[4,80,1024]{2,1,0:T(8,128)(2,1)S(1)}) custom-call(bf16[80,1024]{1,0:T(8,128)(2,1)S(1)} %pad.15.hid, bf16[128,1024]{1,0:T(8,128)(2,1)S(1)} %bitcast.48, bf16[80,1024]{1,0:T(8,128)(2,1)S(1)} %pad.16.og, ...), custom_call_target="tpu_custom_call" | custom-call | tf_op jit(solution)/shard_map/gather/pallas_call | solution.py:154
  39.6 0.0 copy-start.3
  39.6 1.0 copy-done.3
  40.7 0.9 copy-done.4
  41.6 0.8 copy-done.10
  42.4 2.2 %gather_fusion = bf16[4,128,1024]{2,1,0:T(8,128)(2,1)S(1)} fusion(bf16[8,128,1024]{2,1,0:T(8,128)(2,1)} %get-tuple-element.23, s32[1024]{0:T(1024)S(1)} %pad_clamp_fusion.1), kind=kCustom, calls=%fused_computation | custom fusion | bytes 2097168 | tf_op jit(solution)/shard_map/jit(_take)/gather | solution.py:408
  44.6 0.0 copy-start.19
  44.6 1.6 gather.16
  46.2 2.4 %fusion.1 = bf16[4,512,256]{2,1,0:T(8,128)(2,1)} fusion(bf16[512,4,256]{2,1,0:T(4,128)(2,1)} %gather.16, pred[512]{0:T(512)(128)(4,1)S(1)} %broadcast_bitcast_fusion), kind=kLoop, calls=%fused_computation.10 | loop fusion | flops 524288 | bytes 2097664 | tf_op jit(solution)/shard_map/transpose | solution.py:413
  48.6 0.0 copy-done.19
  48.6 5.3 %all-to-all-start.1 = ((bf16[4,512,256]{2,1,0:T(8,128)(2,1)}), bf16[4,512,256]{2,1,0:T(8,128)(2,1)S(1)}, u32[]{:S(2)}, u32[]{:S(2)}) async-start(bf16[4,512,256]{2,1,0:T(8,128)(2,1)} %fusion.1), calls=%async_computation.1 | async-start | bytes 2097152 | tf_op jit(solution)/shard_map/all_to_all | solution.py:412
  53.9 2.4 %bitcast_select_fusion = bf16[512,1024]{1,0:T(8,128)(2,1)} fusion(bf16[4,128,1024]{2,1,0:T(8,128)(2,1)} %copy-done.19, pred[512]{0:T(512)(128)(4,1)S(1)} %broadcast_bitcast_fusion), kind=kLoop, calls=%fused_computation.8 | loop fusion | flops 524288 | bytes 2097664 | tf_op jit(solution)/shard_map/jit(_take)/select_n | solution.py:408
  56.2 1.0 dynamic-slice_bitcast_fusion.q
  57.2 3.7 %copy.15 = bf16[4,2,80,1024]{3,1,2,0:T(2,128)(2,1)} copy(bf16[4,2,80,1024]{3,2,1,0:T(8,128)(2,1)} %bitcast.46) | data formatting | bytes 2621440 | tf_op jit(solution)/shard_map/reshape | solution.py:410
  61.0 0.0 copy-done.20
  61.0 3.8 %convolution_convert_fusion.1.value = bf16[512,1024]{1,0:T(8,128)(2,1)} fusion(bf16[512,1024]{1,0:T(8,128)(2,1)S(1)} %copy-done.20, bf16[1024,1024]{1,0:T(8,128)(2,1)} %param.12), kind=kOutput, calls=%fused_computation.5 | convolution fusion | flops 1074266112 | bytes 4194304 | tf_op jit(solution)/shard_map/dot_general | solution.py:416
  64.8 0.0 copy-done
  64.8 2.2 %convolution_convert_fusion.2.key = bf16[512,1024]{1,0:T(8,128)(2,1)} fusion(bf16[512,1024]{1,0:T(8,128)(2,1)S(1)} %copy-done.20, bf16[1024,1024]{1,0:T(8,128)(2,1)S(1)} %copy-done), kind=kOutput, calls=%fused_computation.6 | convolution fusion | flops 1074266112 | bytes 4194304 | tf_op jit(solution)/shard_map/dot_general | solution.py:415
  67.0 10.5 %attention.1 = (bf16[80,1024]{1,0:T(8,128)(2,1)S(1)}, bf16[80,1024]{1,0:T(8,128)(2,1)S(1)}, bf16[512,1024]{1,0:T(8,128)(2,1)S(1)}, bf16[512,1024]{1,0:T(8,128)(2,1)S(1)}, bf16[2,8,80,256]{3,2,1,0:T(8,128)(2,1)S(1)}) custom-call(bf16[80,1024]{1,0:T(8,128)(2,1)S(1)} %dynamic-slice_bitcast_fusion.q, bf16[80,1024]{1,0:T(8,128)(2,1)S(1)} %pad.16.og, ...), custom_call_target="tpu_custom_call" | custom-call | tf_op jit(solution)/shard_map/attention/pallas_call | solution.py:204
  77.5 0.0 copy-start.6
  77.6 0.0 copy-start.12
  77.6 0.0 copy-start.17
  77.6 0.0 copy-start.21
  77.6 1.3 fusion.5
  78.9 0.0 copy-done.6
  78.9 0.0 copy-done.12
  78.9 0.0 copy-done.17
  78.9 0.6 copy-done.21
  79.5 2.3 %add_convert_fusion = bf16[512,1024]{1,0:T(8,128)(2,1)} fusion(f32[512,1024]{1,0:T(8,128)S(1)} %fusion.5, bf16[512,1024]{1,0:T(8,128)(2,1)S(1)} %get-tuple-element.28, bf16[1024,1024]{1,0:T(8,128)(2,1)S(1)} %copy-done.21), kind=kOutput, calls=%fused_computation.2 | convolution fusion | flops 1074790400 | bytes 6291456 | tf_op jit(solution)/shard_map/dot_general | solution.py:29
  81.8 0.0 all-to-all-done.1.picks
  81.8 5.1 %all-to-all-start = ((bf16[4,2,80,1024]{3,1,2,0:T(2,128)(2,1)}), bf16[4,2,80,1024]{3,1,2,0:T(2,128)(2,1)}, u32[]{:S(2)}, u32[]{:S(2)}) async-start(bf16[4,2,80,1024]{3,1,2,0:T(2,128)(2,1)} %copy.15), calls=%async_computation | async-start | bytes 2621440 | tf_op jit(solution)/shard_map/all_to_all | solution.py:409
  86.9 0.1 fusion.3
  87.0 2.5 %concatenate.3 = bf16[5,128,1024]{2,1,0:T(8,128)(2,1)} pad(bf16[4,128,1024]{2,1,0:T(8,128)(2,1)} %bitcast.52, bf16[]{:T(256)} %constant.29.clone.1), padding=0_1x0_0x0_0 | pad | bytes 2359298 | tf_op jit(solution)/shard_map/concatenate | solution.py:424
  89.5 0.0 copy-done.1
  89.5 0.6 iota_reduce_fusion
  90.1 3.3 %gather_fusion.1 = bf16[8,128,1024]{2,1,0:T(8,128)(2,1)} fusion(bf16[5,128,1024]{2,1,0:T(8,128)(2,1)} %concatenate.3, s32[1024]{0:T(1024)S(1)} %pad_clamp_fusion), kind=kCustom, calls=%fused_computation.1 | custom fusion | bytes 4194336 | tf_op jit(solution)/shard_map/jit(_take)/gather | solution.py:427
  93.4 3.2 %broadcast_select_fusion.ns = bf16[8,128,1024]{2,1,0:T(8,128)(2,1)} fusion(bf16[8,128,1024]{2,1,0:T(8,128)(2,1)} %gather_fusion.1, pred[8]{0:T(512)(128)(4,1)S(1)} %get-tuple-element.38), kind=kLoop, calls=%fused_computation.3 | loop fusion | flops 1048576 | bytes 4194312 | tf_op jit(solution)/shard_map/jit(_take)/select_n | solution.py:427
  96.6 11.0 %fusion.hs = bf16[8,80,1024]{2,1,0:T(8,128)(2,1)S(1)} fusion(bf16[8,1024,1024]{2,1,0:T(8,128)(2,1)} %bitcast.50, bf16[80,1024]{1,0:T(8,128)(2,1)} %copy-done.6), kind=kOutput, calls=%fused_computation.7 | convolution fusion | flops 1342832640 | bytes 18251776 | tf_op jit(solution)/shard_map/dot_general | solution.py:419
  107.6 0.0 copy-start.7
  107.6 0.9 copy-done.7
  108.5 1.1 copy-done.13
  109.6 61.2 %exchange.1 = (bf16[80,1024]{1,0:T(8,128)(2,1)S(1)}, bf16[128,1024]{1,0:T(8,128)(2,1)S(1)}, bf16[4,2,8,80,256]{4,3,2,1,0:T(8,128)(2,1)}, bf16[4,80,1024]{2,1,0:T(8,128)(2,1)S(1)}) custom-call(bf16[8,80,1024]{2,1,0:T(8,128)(2,1)S(1)} %fusion.hs, bf16[8,128,1024]{2,1,0:T(8,128)(2,1)} %broadcast_select_fusion.ns, bf16[2,8,80,256]{3,2,1,0:T(8,128)(2,1)S(1)} %copy-done.13, ...), custom_call_target="tpu_custom_call" | custom-call | tf_op jit(solution)/shard_map/exchange/pallas_call | solution.py:334
  170.8 0.0 copy-start.8
  170.8 0.8 copy-done.8
  171.7 0.0 copy-done.18
  171.7 0.9 pad_bitcast_fusion
  172.6 0.0 copy-done.15
  172.6 0.0 copy-done.2
  172.6 0.0 copy-done.5
  172.6 0.0 copy-done.11
  172.6 18.5 %weights.1 = (f32[256,1024]{1,0:T(8,128)}, f32[256,1024]{1,0:T(8,128)}) custom-call(bf16[4,2,8,80,256]{4,3,2,1,0:T(8,128)(2,1)} %get-tuple-element.34.sgsh, bf16[4,80,1024]{2,1,0:T(8,128)(2,1)S(1)} %copy-done.5, bf16[4,80,1024]{2,1,0:T(8,128)(2,1)S(1)} %copy-done.11, bf16[4,512,256]{2,1,0:T(8,128)(2,1)S(1)} %copy-done.2), custom_call_target="tpu_custom_call" | custom-call | tf_op jit(solution)/shard_map/weights/pallas_call | solution.py:373
  191.1 0.0 all-to-all-done
  191.1 1.7 copy.17
  192.9 0.0 copy-done.9
  192.9 0.0 copy-start.16
  192.9 5.8 %fusion.6 = f32[2048,1024]{1,0:T(8,128)} fusion(bf16[2048,320]{0,1:T(8,128)(2,1)S(1)} %bitcast.51, bf16[320,1024]{1,0:T(8,128)(2,1)S(1)} %bitcast.47), kind=kOutput, calls=%fused_computation.30 | convolution fusion | flops 1342177280 | bytes 10354688 | tf_op jit(solution)/shard_map/dot_general | solution.py:429
  198.7 0.7 copy.22
  (22 shorter events, 0.1 us)
Async XLA Ops:
  0.6 64.2 %copy-start = (bf16[1024,1024]{1,0:T(8,128)(2,1)S(1)}, bf16[1024,1024]{1,0:T(8,128)(2,1)}, u32[]{:S(2)}) copy-start(bf16[1024,1024]{1,0:T(8,128)(2,1)} %param.11) | copy-start | bytes 6291460
  4.4 1.0 copy-start.14
  39.6 1.1 copy-start.3
  40.7 0.9 copy-start.4
  41.6 0.8 copy-start.10
  44.6 4.0 %copy-start.19 = (bf16[4,128,1024]{2,1,0:T(8,128)(2,1)}, bf16[4,128,1024]{2,1,0:T(8,128)(2,1)S(1)}, u32[]{:S(2)}) copy-start(bf16[4,128,1024]{2,1,0:T(8,128)(2,1)S(1)} %gather_fusion) | copy-start | bytes 3145732
  48.6 33.2 %all-to-all-start.1 = ((bf16[4,512,256]{2,1,0:T(8,128)(2,1)}), bf16[4,512,256]{2,1,0:T(8,128)(2,1)S(1)}, u32[]{:S(2)}, u32[]{:S(2)}) async-start(bf16[4,512,256]{2,1,0:T(8,128)(2,1)} %fusion.1), calls=%async_computation.1 | async-start | bytes 2097152 | tf_op jit(solution)/shard_map/all_to_all | solution.py:412
  56.2 4.8 %copy-start.20 = (bf16[512,1024]{1,0:T(8,128)(2,1)S(1)}, bf16[512,1024]{1,0:T(8,128)(2,1)}, u32[]{:S(2)}) copy-start(bf16[512,1024]{1,0:T(8,128)(2,1)} %bitcast_select_fusion) | copy-start | bytes 3145732
  77.5 1.3 copy-start.6
  77.6 1.3 copy-start.12
  77.6 1.3 copy-start.17
  77.6 1.9 copy-start.21
  81.8 7.7 %copy-start.1 = (bf16[4,512,256]{2,1,0:T(8,128)(2,1)}, bf16[4,512,256]{2,1,0:T(8,128)(2,1)S(1)}, u32[]{:S(2)}) copy-start(bf16[4,512,256]{2,1,0:T(8,128)(2,1)S(1)} %all-to-all-done.1.picks) | copy-start | bytes 3145732
  81.8 109.3 %all-to-all-start = ((bf16[4,2,80,1024]{3,1,2,0:T(2,128)(2,1)}), bf16[4,2,80,1024]{3,1,2,0:T(2,128)(2,1)}, u32[]{:S(2)}, u32[]{:S(2)}) async-start(bf16[4,2,80,1024]{3,1,2,0:T(2,128)(2,1)} %copy.15), calls=%async_computation | async-start | bytes 2621440 | tf_op jit(solution)/shard_map/all_to_all | solution.py:409
  107.6 0.9 copy-start.7
  108.5 1.1 copy-start.13
  109.6 62.0 %copy-start.18 = (bf16[80,1024]{1,0:T(8,128)(2,1)S(1)}, bf16[80,1024]{1,0:T(8,128)(2,1)}, u32[]{:S(2)}) copy-start(bf16[80,1024]{1,0:T(8,128)(2,1)} %copy-done.17) | copy-start | bytes 491524
  109.6 63.0 %copy-start.2 = (bf16[4,512,256]{2,1,0:T(8,128)(2,1)S(1)}, bf16[4,512,256]{2,1,0:T(8,128)(2,1)}, u32[]{:S(2)}) copy-start(bf16[4,512,256]{2,1,0:T(8,128)(2,1)} %copy-done.1) | copy-start | bytes 3145732
  109.6 63.0 %copy-start.5 = (bf16[4,80,1024]{2,1,0:T(8,128)(2,1)S(1)}, bf16[4,80,1024]{2,1,0:T(8,128)(2,1)}, u32[]{:S(2)}) copy-start(bf16[4,80,1024]{2,1,0:T(8,128)(2,1)} %copy-done.4) | copy-start | bytes 1966084
  109.6 63.0 %copy-start.11 = (bf16[4,80,1024]{2,1,0:T(8,128)(2,1)S(1)}, bf16[4,80,1024]{2,1,0:T(8,128)(2,1)}, u32[]{:S(2)}) copy-start(bf16[4,80,1024]{2,1,0:T(8,128)(2,1)} %copy-done.10) | copy-start | bytes 1966084
  170.8 0.8 copy-start.8
  171.6 1.0 copy-start.15
  191.1 1.7 copy-start.9
  192.9 5.8 %copy-start.16 = (bf16[128,1024]{1,0:T(8,128)(2,1)S(1)}, bf16[128,1024]{1,0:T(8,128)(2,1)}, u32[]{:S(2)}) copy-start(bf16[128,1024]{1,0:T(8,128)(2,1)} %copy-done.15) | copy-start | bytes 786436

commit v3 on v2

--- a/solution.py
+++ b/solution.py
@@ -18,7 +18,8 @@
 F32 = jnp.float32
 VMEM = pl.BlockSpec(memory_space=pltpu.VMEM)
 ANY = pl.BlockSpec(memory_space=pl.ANY)
-LIMIT = 50 * 2**20
+LIMIT = 60 * 2**20
+TILE = 256
 
 
 def contract_rows(left, right):
@@ -37,8 +38,8 @@
 
 
 def gather_kernel(
-    n, seqs, hid, nb, og, w_hbm, whole, every, qall, ogall,
-    w, acc, w_sem, h_send, h_recv, n_send, n_recv, z_send, z_recv,
+    n, seqs, slots, hid, nb, og, w_hbm, wk_hbm, wv_hbm, qall, ogall, query, keys, values, ext,
+    w, wk, wv, acc, whole, every, states, w_sem, h_send, h_recv, n_send, n_recv, z_send, z_recv,
 ):
     me = lax.axis_index("tensor")
     row = lax.axis_index("seq")
@@ -46,7 +47,10 @@
     core = lax.rem(me, 2)
     chip = me // 2
     twin = me + 1 - 2 * core
-    depth = hid.shape[1]
+    rows, depth = hid.shape
+    many, wide = states.shape
+    share, cut = many // n, wide // seqs
+    pieces = n * depth // seqs // cut
 
     def peer(k):
         return lax.rem(chip + k, chips) * 2 + core
@@ -54,8 +58,12 @@
     def over(k):
         return lax.rem(row + k, seqs)
 
-    fetch = pltpu.make_async_copy(w_hbm, w, w_sem)
-    fetch.start()
+    fetches = [
+        pltpu.make_async_copy(src, dst, w_sem.at[i])
+        for i, (src, dst) in enumerate(((w_hbm, w), (wk_hbm, wk), (wv_hbm, wv)))
+    ]
+    for fetch in fetches:
+        fetch.start()
     barrier = pltpu.get_barrier_semaphore()
     pl.semaphore_signal(barrier, inc=1, device_id={"tensor": twin}, device_id_type=MESH)
 
@@ -80,6 +88,30 @@
 
     def z_copy(ref, out, lane, k):
         return remote(ref, out.at[row], z_send.at[lane, k], z_recv.at[lane, row], "seq", over(k))
+
+    def token_part(dest):
+        at = (dest * pieces + me) * cut
+        return at // depth, pl.ds(pl.multiple_of(lax.rem(at, depth), cut), cut)
+
+    def state_part(dest):
+        return (
+            pl.ds(pl.multiple_of(me * share, share), share),
+            pl.ds(pl.multiple_of(dest * cut, cut), cut),
+        )
+
+    def token_copy(k):
+        block, cols = token_part(over(k))
+        return remote(
+            whole.at[block, :, cols], ext.at[row, pl.ds(0, rows)],
+            z_send.at[2, k], z_recv.at[2, row], "seq", over(k),
+        )
+
+    def state_copy(k):
+        here, cols = state_part(over(k))
+        return remote(
+            states.at[here, cols], ext.at[row, pl.ds(rows, share)],
+            z_send.at[3, k], z_recv.at[3, row], "seq", over(k),
+        )
 
     @pl.loop(1, chips)
     def _(k):
@@ -97,7 +129,7 @@
     whole[me] = hid[...]
     every[me] = nb[...]
     ogall[row] = og[...]
-    fetch.wait()
+    fetches[0].wait()
 
     def add(index):
         part = w[pl.ds(pl.multiple_of(index * depth, depth), depth), :]
@@ -118,7 +150,15 @@
         arrival(whole, h_send, h_recv, index).wait_recv()
         add(index)
 
-    qall[row] = acc[...].astype(BF)
+    @pl.when(me < pieces)
+    def _():
+        for k in range(1, seqs):
+            token_copy(k).start()
+        block, cols = token_part(row)
+        ext[row, pl.ds(0, rows), :] = whole[block, :, cols]
+
+    query[...] = acc[...].astype(BF)
+    qall[row] = query[...]
     for k in range(1, seqs):
         z_copy(qall.at[row], qall, 1, k).start()
 
@@ -130,6 +170,24 @@
     @pl.loop(0, chips)
     def _(k):
         arrival(every, n_send, n_recv, peer(k) + 1 - 2 * core).wait_recv()
+
+    held = every.shape[1]
+    for i in range(many // R):
+        slot = slots[i]
+        block = every[slot, 0] if held == 1 else every[slot // held, slot % held]
+        states[pl.ds(i * R, R), :] = block
+    for k in range(1, seqs):
+        state_copy(k).start()
+    here, cols = state_part(row)
+    ext[row, pl.ds(rows, share), :] = states[here, cols]
+    for fetch in fetches[1:]:
+        fetch.wait()
+
+    @pl.loop(0, wk.shape[1] // TILE)
+    def _(i):
+        at = pl.ds(pl.multiple_of(i * TILE, TILE), TILE)
+        keys[:, at] = jnp.dot(states[...], wk[:, at], preferred_element_type=F32).astype(BF)
+        values[:, at] = jnp.dot(states[...], wv[:, at], preferred_element_type=F32).astype(BF)
 
     for k in range(1, seqs):
         came = over(k)
@@ -138,6 +196,20 @@
                 out.at[came], out.at[came], z_send.at[lane, 0], z_recv.at[lane, came], "seq", came
             ).wait_recv()
             z_copy(og if lane == 0 else qall.at[row], out, lane, k).wait_send()
+        remote(
+            ext.at[came, pl.ds(rows, share)], ext.at[came, pl.ds(rows, share)],
+            z_send.at[3, 0], z_recv.at[3, came], "seq", came,
+        ).wait_recv()
+        state_copy(k).wait_send()
+
+        @pl.when(me < pieces)
+        def _():
+            remote(
+                ext.at[came, pl.ds(0, rows)], ext.at[came, pl.ds(0, rows)],
+                z_send.at[2, 0], z_recv.at[2, came], "seq", came,
+            ).wait_recv()
+            token_copy(k).wait_send()
+
     for ref, out, send, recv in ((hid, whole, h_send, h_recv), (nb, every, n_send, n_recv)):
         own(ref, out, send, recv, 0, twin).wait_send()
 
@@ -147,30 +219,38 @@
             onward(out, send, recv, k).wait_send()
 
 
-def gather(n, seqs, hid, nb, og, w_query):
+def gather(n, seqs, slots, hid, nb, og, w_query, w_key, w_value):
     rows, depth = hid.shape
     width = w_query.shape[1]
+    many = slots.shape[0] * R
     dma = pltpu.SemaphoreType.DMA
     return pl.pallas_call(
         functools.partial(gather_kernel, n, seqs),
         out_shape=(
-            jax.ShapeDtypeStruct((n, rows, depth), BF),
-            jax.ShapeDtypeStruct((n,) + nb.shape, BF),
             jax.ShapeDtypeStruct((seqs, rows, width), BF),
             jax.ShapeDtypeStruct((seqs, rows, width), BF),
-        ),
-        in_specs=[VMEM, VMEM, VMEM, ANY],
-        out_specs=(VMEM,) * 4,
+            jax.ShapeDtypeStruct((rows, width), BF),
+            jax.ShapeDtypeStruct((many, width), BF),
+            jax.ShapeDtypeStruct((many, width), BF),
+            jax.ShapeDtypeStruct((seqs, rows + many // n, DE // seqs), BF),
+        ),
+        in_specs=[pl.BlockSpec(memory_space=pltpu.SMEM), VMEM, VMEM, VMEM, ANY, ANY, ANY],
+        out_specs=(VMEM,) * 6,
         scratch_shapes=[
             pltpu.VMEM(w_query.shape, BF),
+            pltpu.VMEM(w_key.shape, BF),
+            pltpu.VMEM(w_value.shape, BF),
             pltpu.VMEM((rows, width), F32),
-            dma, dma((n,)), dma((n,)), dma((n,)), dma((n,)), dma((2, seqs)), dma((2, seqs)),
+            pltpu.VMEM((n, rows, depth), BF),
+            pltpu.VMEM((n,) + nb.shape, BF),
+            pltpu.VMEM((many, DE), BF),
+            dma((3,)), dma((n,)), dma((n,)), dma((n,)), dma((n,)), dma((4, seqs)), dma((4, seqs)),
         ],
         compiler_params=pltpu.CompilerParams(
             collective_id=0, has_side_effects=True, vmem_limit_bytes=LIMIT
         ),
         name="gather",
-    )(hid, nb, og, w_query)
+    )(slots, hid, nb, og, w_query, w_key, w_value)
 
 
 def attention_kernel(spans, q, og, key, value, mixed, qg, kg, vg, sgsh):
@@ -222,15 +302,38 @@
 
 
 def exchange_kernel(
-    n, seqs, hs, ns, sgsh, qg, hid, nbr, zall, qgall,
-    h_in, n_in, h_send, h_recv, n_send, n_recv, z_send, z_recv,
+    n, seqs, spans, place, sgsh, qg, kg, vg, q, og, ext, w_hbm, wk_hbm, wv_hbm,
+    hid, nbr, qgall, extall, gk, gv,
+    w, wk, wv, hs, ns, h_in, n_in, terms, zall, prow, picks, kbuf, vbuf,
+    w_sem, p_sem, h_send, h_recv, n_send, n_recv, e_send, e_recv, z_send, z_recv,
 ):
     me = lax.axis_index("tensor")
     row = lax.axis_index("seq")
+    chips = n // 2
+    core = lax.rem(me, 2)
+    chip = me // 2
+    twin = me + 1 - 2 * core
+    rows, width = qg.shape
+    many = kg.shape[0]
+    share, reach = many // n, many // spans
+    depth = hs.shape[2]
+    held = ns.shape[1]
 
     def peer(k):
         return lax.rem(me + k, n)
 
+    def mate(k):
+        return lax.rem(chip + k, chips) * 2 + core
+
+    def tile(i, size=TILE):
+        return pl.ds(pl.multiple_of(i * size, size), size)
+
+    fetches = [
+        pltpu.make_async_copy(src, dst, w_sem.at[i])
+        for i, (src, dst) in enumerate(((wk_hbm, wk), (wv_hbm, wv), (w_hbm, w)))
+    ]
+    for fetch in fetches:
+        fetch.start()
     barrier = pltpu.get_barrier_semaphore()
 
     @pl.loop(1, n)
@@ -246,8 +349,27 @@
     def scatter(ref, into, send, recv, k):
         return remote(ref.at[peer(k)], into.at[me], send.at[k], recv.at[me], "tensor", peer(k))
 
-    outs = (qgall, zall)
-    owns = (qg, sgsh)
+    def spread(k):
+        return remote(
+            ext, extall.at[me], e_send.at[k], e_recv.at[me], "tensor", mate(k)
+        )
+
+    def to_twin():
+        return remote(ext, extall.at[me], e_send.at[0], e_recv.at[me], "tensor", twin)
+
+    def onward(k):
+        return remote(
+            extall.at[mate(k)], extall.at[mate(k)], e_send.at[chips + k], e_recv.at[mate(k)],
+            "tensor", twin,
+        )
+
+    def came(index):
+        return remote(
+            extall.at[index], extall.at[index], e_send.at[0], e_recv.at[index], "tensor", twin
+        )
+
+    outs = (zall, qgall)
+    owns = (sgsh, qg)
 
     def hop(side, h, lane):
         step = 1 - 2 * side
@@ -280,13 +402,95 @@
             for lane in range(2):
                 hop(side, 0, lane).start()
 
+    @pl.loop(1, chips)
+    def _(k):
+        spread(k).start()
+
+    to_twin().start()
+    mine = pltpu.make_async_copy(ext, extall.at[me], p_sem.at[n])
+    mine.start()
+    qgall[row] = qg[...]
+
+    fetches[0].wait()
+    fetches[1].wait()
+
+    @pl.loop(0, wk.shape[0] // TILE)
+    def _(i):
+        part = contract_cols(kg[...], wk[tile(i), :]) + contract_cols(vg[...], wv[tile(i), :])
+        for p in range(many // R):
+            terms[p, :, tile(i)] = part[p * R:(p + 1) * R].astype(BF)
+
+    terms[many // R] = jnp.zeros_like(terms[0])
+
+    @pl.loop(0, n)
+    def _(k):
+        for j in range(held):
+            ns[peer(k), j] = terms[place[peer(k) * held + j]]
+
     @pl.loop(1, n)
     def _(k):
+        scatter(ns, n_in, n_send, n_recv, k).start()
+
+    @pl.loop(1, chips)
+    def _(k):
+        came(mate(k)).wait_recv()
+        onward(k).start()
+
+    fetches[2].wait()
+
+    def hidden_term(index):
+        hs[index] = contract_cols(qg[...], w[tile(index, depth), :]).astype(BF)
+
+    @pl.loop(1, n)
+    def _(k):
+        hidden_term(peer(k))
         scatter(hs, h_in, h_send, h_recv, k).start()
-        scatter(ns, n_in, n_send, n_recv, k).start()
-
-    for lane in range(2):
-        outs[lane][row] = owns[lane][...]
+
+    hidden_term(me)
+
+    @pl.loop(0, chips)
+    def _(k):
+        came(mate(k) + 1 - 2 * core).wait_recv()
+
+    mine.wait()
+
+    def pick_copy(t):
+        at = pl.ds(pl.multiple_of(t * share, share), share)
+        return pltpu.make_async_copy(
+            extall.at[t, :, pl.ds(rows, share)], prow.at[:, at], p_sem.at[t]
+        )
+
+    @pl.loop(0, n)
+    def _(t):
+        pick_copy(t).start()
+
+    @pl.loop(0, n)
+    def _(t):
+        pick_copy(t).wait()
+
+    def add(origin, key_ref, value_ref):
+        picks[...] = prow[origin].T
+
+        @pl.loop(0, width // TILE)
+        def _(i):
+            gk[:, tile(i)] += jnp.dot(picks[...], key_ref[:, tile(i)], preferred_element_type=F32)
+            gv[:, tile(i)] += jnp.dot(picks[...], value_ref[:, tile(i)], preferred_element_type=F32)
+
+    def rebuild(origin):
+        @pl.loop(0, width // HS)
+        def _(h):
+            for lane, right, out in ((0, q, kbuf), (1, og, vbuf)):
+                for u in range(spans):
+                    here = pl.ds(u * SPAN, SPAN if u < spans - 1 else TAIL)
+                    out[pl.ds(u * reach, reach), tile(h, HS)] = contract_rows(
+                        zall[origin, lane, h, here, :], right[origin, here, tile(h, HS)]
+                    ).astype(BF)
+
+        add(origin, kbuf, vbuf)
+
+    gk[...] = jnp.zeros_like(gk)
+    gv[...] = jnp.zeros_like(gv)
+    add(row, kg, vg)
     for h in range(seqs - 1):
         for lane in range(2):
             for side in range(2):
@@ -299,22 +503,26 @@
                     def _():
                         hop(side, h + 1, lane).start()
 
-        if h == 0:
-            for ref, into, send, recv, out in (
-                (hs, h_in, h_send, h_recv, hid), (ns, n_in, n_send, n_recv, nbr)
-            ):
-                @pl.loop(1, n)
-                def _(k):
-                    remote(
-                        into.at[peer(k)], into.at[peer(k)], send.at[0], recv.at[peer(k)],
-                        "tensor", peer(k),
-                    ).wait_recv()
-
-                into[me] = ref[me]
-                total = into[0].astype(F32)
-                for j in range(1, n):
-                    total = total + into[j].astype(F32)
-                out[...] = total.astype(BF)
+        for side in range(2):
+            @pl.when(arrives(side, h))
+            def _():
+                rebuild(row - (1 - 2 * side) * (h + 1))
+
+    for ref, into, send, recv, out in (
+        (ns, n_in, n_send, n_recv, nbr), (hs, h_in, h_send, h_recv, hid)
+    ):
+        @pl.loop(1, n)
+        def _(k):
+            remote(
+                into.at[peer(k)], into.at[peer(k)], send.at[0], recv.at[peer(k)],
+                "tensor", peer(k),
+            ).wait_recv()
+
+        into[me] = ref[me]
+        total = into[0].astype(F32)
+        for j in range(1, n):
+            total = total + into[j].astype(F32)
+        out[...] = total.astype(BF)
 
     for side in range(2):
         for h in range(seqs - 1):
@@ -323,66 +531,60 @@
                 for lane in range(2):
                     hop(side, h, lane).wait_send()
 
+    to_twin().wait_send()
+
+    @pl.loop(1, chips)
+    def _(k):
+        spread(k).wait_send()
+        onward(k).wait_send()
+
     @pl.loop(1, n)
     def _(k):
         scatter(hs, h_in, h_send, h_recv, k).wait_send()
         scatter(ns, n_in, n_send, n_recv, k).wait_send()
 
 
-def exchange(n, seqs, hs, ns, sgsh, qg):
+def exchange(n, seqs, spans, held, place, sgsh, qg, kg, vg, q, og, ext, w_query, w_key, w_value):
     dma = pltpu.SemaphoreType.DMA
+    rows, width = qg.shape
+    many = kg.shape[0]
+    depth = w_query.shape[0] // n
+    cut = DE // seqs
     return pl.pallas_call(
-        functools.partial(exchange_kernel, n, seqs),
+        functools.partial(exchange_kernel, n, seqs, spans),
         out_shape=(
-            jax.ShapeDtypeStruct(hs.shape[1:], BF),
-            jax.ShapeDtypeStruct(ns.shape[1:], BF),
-            jax.ShapeDtypeStruct((seqs,) + sgsh.shape, BF),
-            jax.ShapeDtypeStruct((seqs,) + qg.shape, BF),
-        ),
-        in_specs=[VMEM] * 4,
-        out_specs=(VMEM,) * 4,
+            jax.ShapeDtypeStruct((rows, depth), BF),
+            jax.ShapeDtypeStruct((held, R, DE), BF),
+            jax.ShapeDtypeStruct((seqs, rows, width), BF),
+            jax.ShapeDtypeStruct((n,) + ext.shape, BF),
+            jax.ShapeDtypeStruct((cut, width), F32),
+            jax.ShapeDtypeStruct((cut, width), F32),
+        ),
+        in_specs=[pl.BlockSpec(memory_space=pltpu.SMEM)] + [VMEM] * 7 + [ANY] * 3,
+        out_specs=(VMEM, VMEM, VMEM, ANY, VMEM, VMEM),
         scratch_shapes=[
-            pltpu.VMEM(hs.shape, BF), pltpu.VMEM(ns.shape, BF),
-            dma((n,)), dma((n,)), dma((n,)), dma((n,)),
+            pltpu.VMEM(w_query.shape, BF),
+            pltpu.VMEM(w_key.shape, BF),
+            pltpu.VMEM(w_value.shape, BF),
+            pltpu.VMEM((n, rows, depth), BF),
+            pltpu.VMEM((n, held, R, DE), BF),
+            pltpu.VMEM((n, rows, depth), BF),
+            pltpu.VMEM((n, held, R, DE), BF),
+            pltpu.VMEM((many // R + 1, R, DE), BF),
+            pltpu.VMEM((seqs,) + sgsh.shape, BF),
+            pltpu.VMEM((seqs, many, cut), BF),
+            pltpu.VMEM((cut, many), BF),
+            pltpu.VMEM((many, width), BF),
+            pltpu.VMEM((many, width), BF),
+            dma((3,)), dma((n + 1,)),
+            dma((n,)), dma((n,)), dma((n,)), dma((n,)), dma((n,)), dma((n,)),
             dma((2, seqs - 1, 2)), dma((2, seqs - 1, 2)),
         ],
         compiler_params=pltpu.CompilerParams(
             collective_id=1, has_side_effects=True, vmem_limit_bytes=LIMIT
         ),
         name="exchange",
-    )(hs, ns, sgsh, qg)
-
-
-def weight_kernel(spans, seqs, sgsh, q, og, picks, wk, wv):
-    reach = sgsh.shape[-1]
-    for lane, right, out in ((0, q, wk), (1, og, wv)):
-        total = jnp.zeros(out.shape, F32)
-        for s in range(seqs):
-            for u in range(spans):
-                here = pl.ds(u * SPAN, SPAN if u < spans - 1 else TAIL)
-                grad = contract_rows(sgsh[s, lane, 0, here, :], right[s, here, :]).astype(BF)
-                total += contract_rows(picks[s, pl.ds(u * reach, reach), :], grad)
-        out[...] = total
-
-
-def weights(spans, sgsh, q, og, picks):
-    seqs, _, heads, rows, reach = sgsh.shape
-    cols = picks.shape[2]
-    narrow = pl.BlockSpec((seqs, rows, HS), lambda h: (0, 0, h))
-    result = jax.ShapeDtypeStruct((cols, heads * HS), F32)
-    return pl.pallas_call(
-        functools.partial(weight_kernel, spans, seqs),
-        grid=(heads,),
-        out_shape=(result, result),
-        in_specs=[
-            pl.BlockSpec((seqs, 2, 1, rows, reach), lambda h: (0, 0, h, 0, 0)),
-            narrow, narrow,
-            pl.BlockSpec(picks.shape, lambda h: (0, 0, 0)),
-        ],
-        out_specs=(pl.BlockSpec((cols, HS), lambda h: (0, h)),) * 2,
-        compiler_params=pltpu.CompilerParams(vmem_limit_bytes=LIMIT),
-        name="weights",
-    )(sgsh, q, og, picks)
+    )(place, sgsh, qg, kg, vg, q, og, ext, w_query, w_key, w_value)
 
 
 def body(n, seqs, hidden, neighbours, slot_of, w_query, w_key, w_value, out_grad):
@@ -401,41 +603,25 @@
         return jnp.pad(x[: length - lag], ((lag, 0), (0, 0)))[None]
 
     og = later(out_grad[0])
-    row = lax.axis_index("seq")
-    whole, every, qall, ogall = gather(
-        n, seqs, later(hidden[0]), neighbours[0].reshape(slot_count * R, DE), og, w_query
+    qall, ogall, query, keys, values, ext = gather(
+        n, seqs, slots, later(hidden[0]), neighbours[0], og, w_query, w_key, w_value
     )
-    states = jnp.take(every.reshape(-1, R, DE), slots, axis=0).reshape(-1, DE)
-    tokens_all = lax.all_to_all(
-        whole.reshape((seqs, n // seqs) + whole.shape[1:]), "seq", 0, 0, tiled=True
+    mixed, qg, kg, vg, sgsh = attention(spans, query, og, keys, values)
+    wanted = lax.iota(jnp.int32, slot_count * n)[:, None] == slots[None, :]
+    nth = lax.iota(jnp.int32, slots.shape[0])[None, :] - slots.shape[0]
+    place = jnp.sum(jnp.where(wanted, nth, 0), 1) + slots.shape[0]
+    hid, nbr, qgall, extall, wk, wv = exchange(
+        n, seqs, spans, slot_count, place, sgsh, qg, kg, vg, qall, ogall, ext,
+        w_query, w_key, w_value,
     )
-    picks = lax.all_to_all(
-        states.reshape(-1, seqs, DE // seqs).transpose(1, 0, 2), "seq", 0, 0, tiled=True
-    )
-    keys = jnp.dot(states, w_key, preferred_element_type=F32).astype(BF)
-    values = jnp.dot(states, w_value, preferred_element_type=F32).astype(BF)
-    query = lax.dynamic_index_in_dim(qall, row, 0, keepdims=False)
-    mixed, qg, kg, vg, sgsh = attention(spans, query, og, keys, values)
-    feature_terms = lax.dot_general(
-        w_query.reshape(n, -1, width), qg, (((2,), (1,)), ((), ())), preferred_element_type=F32
-    ).astype(BF)
-    feature_terms = feature_terms.transpose(0, 2, 1)
-    terms = (contract_cols(kg, w_key) + contract_cols(vg, w_value)).astype(BF)
-    terms = jnp.concatenate([terms.reshape(-1, R, DE), jnp.zeros((1, R, DE), BF)], 0)
-    wanted = lax.iota(jnp.int32, slot_count * n)[:, None] == slots[None, :]
-    place = jnp.where(wanted.any(1), jnp.argmax(wanted, 1).astype(jnp.int32), slots.shape[0])
-    placed = jnp.take(terms, place, axis=0).reshape(n, slot_count * R, DE)
-    hid, nbr, zall, qgall = exchange(n, seqs, feature_terms, placed, sgsh, qg)
+    pieces = w_query.shape[0] // seqs // ext.shape[2]
     query_part = lax.dot_general(
-        tokens_all.transpose(1, 3, 0, 2).reshape(-1, seqs * rows),
+        extall[:pieces, :, :rows].transpose(0, 3, 1, 2).reshape(-1, seqs * rows),
         qgall.reshape(seqs * rows, width),
         (((1,), (0,)), ((), ())),
         preferred_element_type=F32,
     )
-    wk, wv = weights(spans, zall, qall, ogall, picks)
-    return (
-        back(mixed), back(hid), nbr.reshape(1, slot_count, R, DE), query_part, wk, wv
-    )
+    return (back(mixed), back(hid), nbr[None], query_part, wk, wv)
 
 
 def solution(mesh):

time: 202 us -> 144 us (0.71); the launches traced: 199 us -> 144 us
  matrix products: 26.4 us -> 5.78 us
  local copies, waits for them, and re-layouts: 28.6 us -> 10.7 us
  starting transfers between devices: 10.3 us -> 0 us
  other arithmetic: 8.65 us -> 0.61 us
    dot_general x6 -> x1, matrix products: 26.4 us -> 5.78 us  [body(): lax.dot_general(extall[:pieces, :, :rows].transpose(0, 3, 1, 2).reshape(-...]
    pallas_call x1, Pallas kernels: 34.3 us -> 44.7 us  [gather(): pl.pallas_call(functools.partial(gather_kernel, n, seqs), out_shape=(jax....]
    all_to_all x2 -> x0, starting transfers between devices: 10.3 us -> none  [the longest x1 5.25 us: body(): lax.all_to_all(states.reshape(-1, seqs, DE // seqs).transpose(1, 0, 2), '...]
    pallas_call x2 -> x1, Pallas kernels: 79.7 us -> 70.5 us  [exchange(): pl.pallas_call(functools.partial(exchange_kernel, n, seqs, spans), out_sh...]
    gather x3 -> x0, local copies, waits for them, and re-layouts: 7.1 us -> none  [the longest x2 3.78 us: body(): states = jnp.take(every.reshape(-1, R, DE), slots, axis=0).reshape(-1, DE)]
    unnamed x46 -> x18, local copies, waits for them, and re-layouts: 9.65 us -> 3.07 us
    select_n x3 -> x0, other arithmetic: 5.53 us -> none  [the longest x1 3.17 us: body(): placed = jnp.take(terms, place, axis=0).reshape(n, slot_count * R, DE)]
    reshape x1 -> x0, local copies, waits for them, and re-layouts: 3.74 us -> none  [body(): whole.reshape((seqs, n // seqs) + whole.shape[1:])]
  transfers between devices with their start and end apart: 2 -> 0, of which waited for: 0 -> 0; matrix products, arithmetic and copies ran while one was open for 19% -> 0% of each run, Pallas kernels for 45% -> 0%
where the time goes in v3:
time: 144 us
  Pallas kernels  126 us (88%)
  local copies, waits for them, and re-layouts  10.7 us (7%)
  matrix products  5.78 us (4%)
    pallas_call x1, Pallas kernels, exchange(): pl.pallas_call(functools.partial(exchange_kernel, n, seqs, spans), out_sh...  70.5 us
    pallas_call x1, Pallas kernels, gather(): pl.pallas_call(functools.partial(gather_kernel, n, seqs), out_shape=(jax....  44.7 us
    pallas_call x1, Pallas kernels, attention(): pl.pallas_call(functools.partial(attention_kernel, spans), grid=(heads,),...  10.5 us
    dot_general x1, matrix products, body(): lax.dot_general(extall[:pieces, :, :rows].transpose(0, 3, 1, 2).reshape(-...  5.78 us
    unnamed x18, local copies, waits for them, and re-layouts  3.07 us

profile of v3, /device:TPU:0, one launch (start us, length us, event | category | flops | bytes accessed | tf_op | source)
XLA Modules:
  0.0 143.6 jit_solution(9177631808424930186)
XLA Ops:
  0.6 0.9 slice_bitcast_fusion.1
  1.6 0.7 pad.15.og
  2.3 1.4 reshape_squeeze.3.slots
  3.6 0.9 slice_bitcast_fusion.2
  4.6 0.7 pad.14.hid
  5.2 44.7 %gather.1 = (bf16[4,80,1024]{2,1,0:T(8,128)(2,1)}, bf16[4,80,1024]{2,1,0:T(8,128)(2,1)}, bf16[80,1024]{1,0:T(8,128)(2,1)}, bf16[512,1024]{1,0:T(8,128)(2,1)}, bf...) custom-call(s32[4]{0:T(128)} %reshape_squeeze.3.slots, bf16[80,1024]{1,0:T(8,128)(2,1)} %pad.14.hid, ...), custom_call_target="tpu_custom_call" | custom-call | tf_op jit(solution)/shard_map/gather/pallas_call | solution.py:227
  49.9 0.0 copy-start.6
  49.9 10.5 %attention.1 = (bf16[80,1024]{1,0:T(8,128)(2,1)}, bf16[80,1024]{1,0:T(8,128)(2,1)}, bf16[512,1024]{1,0:T(8,128)(2,1)}, bf16[512,1024]{1,0:T(8,128)(2,1)}, bf16[2,8,80,256]{3,2,1,0:T(8,128)(2,1)}) custom-call(bf16[80,1024]{1,0:T(8,128)(2,1)} %get-tuple-element.23.q, bf16[80,1024]{1,0:T(8,128)(2,1)} %pad.15.og, bf16[512,1024]{1,0:T(8,128)(2,1)} %get-tuple-element.24.key, ...), custom_call_target="tpu_custom_call" | custom-call | tf_op jit(solution)/shard_map/attention/pallas_call | solution.py:284
  60.5 0.0 copy-done.6
  60.5 0.1 select_reduce_fusion
  60.6 0.5 broadcast_add_fusion.place
  61.1 70.5 %exchange.1 = (bf16[80,1024]{1,0:T(8,128)(2,1)}, bf16[1,128,1024]{2,1,0:T(8,128)(2,1)}, bf16[4,80,1024]{2,1,0:T(8,128)(2,1)}, bf16[8,4,144,256]{3,2,1,0:T(8,128)...) custom-call(s32[8]{0:T(128)} %broadcast_add_fusion.place, bf16[2,8,80,256]{3,2,1,0:T(8,128)(2,1)} %get-tuple-element.27.sgsh, ...), custom_call_target="tpu_custom_call" | custom-call | tf_op jit(solution)/shard_map/exchange/pallas_call | solution.py:553
  131.6 1.4 slice_bitcast_fusion
  133.1 0.0 copy-start.2
  133.1 0.7 copy.14
  133.8 0.4 copy.15
  134.2 0.0 copy-done.2
  134.2 0.0 copy-start.5
  134.2 0.0 copy-start.4
  134.2 0.0 copy-start.3
  134.3 0.0 copy-start.1
  134.3 5.8 %fusion = f32[2048,1024]{1,0:T(8,128)} fusion(bf16[2048,320]{0,1:T(8,128)(2,1)S(1)} %bitcast.20, bf16[320,1024]{1,0:T(8,128)(2,1)S(1)} %bitcast.22), kind=kOutput, calls=%fused_computation.9 | convolution fusion | flops 1342177280 | bytes 10354688 | tf_op jit(solution)/shard_map/dot_general | solution.py:618
  140.0 0.0 copy-start
  140.0 0.0 copy-done.5
  140.1 0.0 copy-done.4
  140.1 0.9 pad_bitcast_fusion
  141.0 0.0 copy-done.3
  141.0 0.7 copy.19
  141.7 0.0 copy-done.1
  141.7 1.0 copy.20
  142.6 0.0 copy-done
  142.7 1.0 copy.21
  (3 shorter events, 0.0 us)
Async XLA Ops:
  49.9 10.5 %copy-start.6 = (s32[4]{0:T(128)S(1)}, s32[4]{0:T(128)}, u32[]{:S(2)}) copy-start(s32[4]{0:T(128)} %reshape_squeeze.3.slots) | copy-start | bytes 52
  133.1 1.2 copy-start.2
  134.2 5.8 %copy-start.5 = (bf16[80,1024]{1,0:T(8,128)(2,1)S(1)}, bf16[80,1024]{1,0:T(8,128)(2,1)}, u32[]{:S(2)}) copy-start(bf16[80,1024]{1,0:T(8,128)(2,1)} %get-tuple-element.34) | copy-start | bytes 491524
  134.2 5.8 %copy-start.4 = (bf16[80,1024]{1,0:T(8,128)(2,1)S(1)}, bf16[80,1024]{1,0:T(8,128)(2,1)}, u32[]{:S(2)}) copy-start(bf16[80,1024]{1,0:T(8,128)(2,1)} %get-tuple-element.26) | copy-start | bytes 491524
  134.2 6.7 %copy-start.3 = (bf16[1,128,1024]{2,1,0:T(8,128)(2,1)S(1)}, bf16[1,128,1024]{2,1,0:T(8,128)(2,1)}, u32[]{:S(2)}) copy-start(bf16[1,128,1024]{2,1,0:T(8,128)(2,1)} %get-tuple-element.35) | copy-start | bytes 786436
  134.3 7.4 %copy-start.1 = (f32[256,1024]{1,0:T(8,128)S(1)}, f32[256,1024]{1,0:T(8,128)}, u32[]{:S(2)}) copy-start(f32[256,1024]{1,0:T(8,128)} %get-tuple-element.52) | copy-start | bytes 3145732
  140.0 2.6 %copy-start = (f32[256,1024]{1,0:T(8,128)S(1)}, f32[256,1024]{1,0:T(8,128)}, u32[]{:S(2)}) copy-start(f32[256,1024]{1,0:T(8,128)} %get-tuple-element.53) | copy-start | bytes 3145732

commit v4 on v1

v4 whole, which is shorter than its diff:
```python
import functools
import math

import jax
import jax.numpy as jnp
from jax import lax
from jax.experimental import pallas as pl
from jax.experimental.pallas import tpu as pltpu
from jax.sharding import PartitionSpec as P

HS = 128
DE = 1024
SPAN = 64
R = 128
TAIL = 16
MESH = pl.DeviceIdType.MESH
BF = jnp.bfloat16
F32 = jnp.float32
VMEM = pl.BlockSpec(memory_space=pltpu.VMEM)
ANY = pl.BlockSpec(memory_space=pl.ANY)
LIMIT = 63 * 2**20
TILE = 256


def contract_rows(left, right):
    return lax.dot_general(left, right, (((0,), (0,)), ((), ())), preferred_element_type=F32)


def contract_cols(left, right):
    return lax.dot_general(left, right, (((1,), (1,)), ((), ())), preferred_element_type=F32)


def remote(src, dst, send, recv, axis, index):
    return pltpu.make_async_remote_copy(
        src_ref=src, dst_ref=dst, send_sem=send, recv_sem=recv,
        device_id={axis: index}, device_id_type=MESH,
    )


def kernel(
    n, seqs, spans, slots, hid_in, nb, og_in, w_hbm, wk_hbm, wv_hbm,
    mixed, hid_out, nbr, qgall, extall, gk, gv,
    w, wk, wv, acc, hid, whole, every, states, keys, values, kg, vg, qall, ogall, ext,
    h_in, n_in, terms, zall, picks,
    w_sem, p_sem, h_send, h_recv, n_send, n_recv, z_send, z_recv,
    e_send, e_recv, hs_send, hs_recv, ns_send, ns_recv, line_send, line_recv,
):
    me = lax.axis_index("tensor")
    row = lax.axis_index("seq")
    chips = n // 2
    core = lax.rem(me, 2)
    chip = me // 2
    twin = me + 1 - 2 * core
    rows, depth = hid.shape
    _, many, cut = states.shape
    width = acc.shape[1]
    heads = width // HS
    share, reach = many // n, many // spans
    pieces = n * depth // seqs // cut
    blocks = many // R
    held = every.shape[1]
    near = slots.shape[1]
    scale = 1.0 / math.sqrt(HS)

    def mate(k):
        return lax.rem(chip + k, chips) * 2 + core

    def peer(k):
        return lax.rem(me + k, n)

    def over(k):
        return lax.rem(row + k, seqs)

    def tile(i, size=TILE):
        return pl.ds(pl.multiple_of(i * size, size), size)

    def slot_at(i):
        return slots[i // near, i % near]

    fetches = [
        pltpu.make_async_copy(src, dst, w_sem.at[i])
        for i, (src, dst) in enumerate(((w_hbm, w), (wk_hbm, wk), (wv_hbm, wv)))
    ]
    for fetch in fetches:
        fetch.start()
    barrier = pltpu.get_barrier_semaphore()

    @pl.loop(1, n)
    def _(k):
        pl.semaphore_signal(barrier, inc=1, device_id={"tensor": peer(k)}, device_id_type=MESH)

    for k in range(1, seqs):
        pl.semaphore_signal(barrier, inc=1, device_id={"seq": over(k)}, device_id_type=MESH)

    length = hid_in.shape[0]
    for ref, out in ((hid_in, hid), (og_in, ogall.at[row])):
        whole_rows = ref[pl.ds(length - rows, rows), :].astype(F32)
        moved = pltpu.roll(whole_rows, rows - (SPAN - 1 - (length - rows)), 0)
        at = lax.broadcasted_iota(jnp.int32, moved.shape, 0)
        out[...] = jnp.where(at < length - SPAN + 1, moved, 0.0).astype(BF)
    pl.semaphore_wait(barrier, n - 1 + seqs - 1)

    def own(ref, out, send, recv, k, target):
        return remote(ref, out.at[me], send.at[k], recv.at[me], "tensor", target)

    def onward(out, send, recv, k):
        return remote(
            out.at[mate(k)], out.at[mate(k)], send.at[chips + k], recv.at[mate(k)], "tensor", twin
        )

    def arrival(out, send, recv, index):
        return remote(out.at[index], out.at[index], send.at[0], recv.at[index], "tensor", twin)

    def spread(ref, out, send, recv):
        @pl.loop(1, chips)
        def _(k):
            own(ref, out, send, recv, k, mate(k)).start()

        own(ref, out, send, recv, 0, twin).start()

    def pass_on(out, send, recv, use=None):
        @pl.loop(1, chips)
        def _(k):
            arrival(out, send, recv, mate(k)).wait_recv()
            onward(out, send, recv, k).start()
            if use is not None:
                use(mate(k))

    def rest(out, send, recv, use=None):
        @pl.loop(0, chips)
        def _(k):
            index = mate(k) + 1 - 2 * core
            arrival(out, send, recv, index).wait_recv()
            if use is not None:
                use(index)

    def sent(ref, out, send, recv):
        own(ref, out, send, recv, 0, twin).wait_send()

        @pl.loop(1, chips)
        def _(k):
            own(ref, out, send, recv, k, mate(k)).wait_send()
            onward(out, send, recv, k).wait_send()

    def z_copy(out, lane, k):
        return remote(
            out.at[row], out.at[row], z_send.at[lane, k], z_recv.at[lane, row], "seq", over(k)
        )

    def token_part(dest):
        at = (dest * pieces + me) * cut
        return at // depth, pl.ds(pl.multiple_of(lax.rem(at, depth), cut), cut)

    def state_part(dest):
        return dest, tile(me, share)

    def token_copy(k):
        block, cols = token_part(over(k))
        return remote(
            whole.at[block, :, cols], ext.at[row, pl.ds(0, rows)],
            z_send.at[2, k], z_recv.at[2, row], "seq", over(k),
        )

    def state_copy(k):
        return remote(
            states.at[state_part(over(k))], ext.at[row, pl.ds(rows, share)],
            z_send.at[3, k], z_recv.at[3, row], "seq", over(k),
        )

    def z_came(ref, lane, index):
        return remote(ref, ref, z_send.at[lane, 0], z_recv.at[lane, index], "seq", index)

    spread(hid, whole, h_send, h_recv)
    spread(nb, every, n_send, n_recv)
    for k in range(1, seqs):
        z_copy(ogall, 0, k).start()
    whole[me] = hid[...]
    every[me] = nb[...]
    fetches[0].wait()

    def project(index):
        acc[...] += jnp.dot(whole[index], w[tile(index, depth), :], preferred_element_type=F32)

    acc[...] = jnp.zeros_like(acc)
    project(me)
    pass_on(whole, h_send, h_recv, project)
    rest(whole, h_send, h_recv, project)

    @pl.when(me < pieces)
    def _():
        for k in range(1, seqs):
            token_copy(k).start()
        block, cols = token_part(row)
        ext[row, pl.ds(0, rows), :] = whole[block, :, cols]

    qall[row] = acc[...].astype(BF)
    pass_on(every, n_send, n_recv)
    rest(every, n_send, n_recv)
    for i in range(blocks):
        slot = slot_at(i)
        block = every[slot, 0] if held == 1 else every[slot // held, slot % held]
        for part in range(seqs):
            states[part, pl.ds(i * R, R), :] = block[:, part * cut:(part + 1) * cut]
    for k in range(1, seqs):
        state_copy(k).start()
    for k in range(1, seqs):
        z_copy(qall, 1, k).start()
    ext[row, pl.ds(rows, share), :] = states[row, tile(me, share), :]
    for fetch in fetches[1:]:
        fetch.wait()

    @pl.loop(0, width // TILE)
    def _(i):
        for out, weight in ((keys, wk), (values, wv)):
            total = jnp.zeros((many, TILE), F32)
            for part in range(seqs):
                total += jnp.dot(
                    states[part], weight[pl.ds(part * cut, cut), tile(i)],
                    preferred_element_type=F32,
                )
            out[:, tile(i)] = total.astype(BF)

    def lane_ref(origin, lane):
        if isinstance(lane, int) and lane == heads:
            return qgall.at[origin]
        return zall.at[origin, lane]

    def hop(side, h, lane):
        step = 1 - 2 * side
        ref = lane_ref(row - step * h, lane)
        return remote(
            ref, ref, line_send.at[side, h, lane], line_recv.at[side, h, lane], "seq", row + step
        )

    def sends(side, h):
        if side == 0:
            return (row - h >= 0) & (row + 1 < seqs)
        return (row + h < seqs) & (row >= 1)

    def arrives(side, h):
        return row - 1 - h >= 0 if side == 0 else row + 1 + h < seqs

    def arrived(side, h, lane):
        step = 1 - 2 * side
        ref = lane_ref(row - step * (h + 1), lane)
        return remote(
            ref, ref, line_send.at[side, h, lane], line_recv.at[side, h, lane], "seq", row - step
        )

    def push(lane):
        for side in range(2):
            @pl.when(sends(side, 0))
            def _():
                hop(side, 0, lane).start()

    def relay(h, lane):
        for side in range(2):
            @pl.when(arrives(side, h))
            def _():
                arrived(side, h, lane).wait_recv()

            if h + 1 < seqs - 1:
                @pl.when(sends(side, h + 1))
                def _():
                    hop(side, h + 1, lane).start()

    @pl.loop(0, heads)
    def _(h):
        at = tile(h, HS)
        for u in range(spans):
            here = pl.ds(u * SPAN, SPAN if u < spans - 1 else TAIL)
            tall = pl.ds(u * reach, reach)
            qu, gu = qall[row, here, at], ogall[row, here, at]
            ku, vu = keys[tall, at], values[tall, at]
            raised = jnp.exp(contract_cols(qu, ku) * scale)
            shares = raised / jnp.sum(raised, axis=-1, keepdims=True)
            share_bf = shares.astype(BF)
            mixed[here, at] = jnp.dot(share_bf, vu, preferred_element_type=F32).astype(BF)
            share_grad = contract_cols(gu, vu)
            centre = jnp.sum(shares * share_grad, axis=-1, keepdims=True)
            score_grad = (shares * (share_grad - centre) * scale).astype(BF)
            qgall[row, here, at] = jnp.dot(
                score_grad, ku, preferred_element_type=F32
            ).astype(BF)
            kg[tall, at] = contract_rows(score_grad, qu).astype(BF)
            vg[tall, at] = contract_rows(share_bf, gu).astype(BF)
            zall[row, h, 0, here, :] = score_grad
            zall[row, h, 1, here, :] = share_bf
        push(h)

    push(heads)

    for k in range(1, seqs):
        came = over(k)
        z_came(ext.at[came, pl.ds(rows, share)], 3, came).wait_recv()

        @pl.when(me < pieces)
        def _():
            z_came(ext.at[came, pl.ds(0, rows)], 2, came).wait_recv()
            token_copy(k).wait_send()

        state_copy(k).wait_send()

    spread(ext, extall, e_send, e_recv)
    mine = pltpu.make_async_copy(ext, extall.at[me], p_sem.at[n])
    mine.start()
    sent(hid, whole, h_send, h_recv)
    sent(nb, every, n_send, n_recv)

    def scatter(ref, into, send, recv, k):
        return remote(ref.at[peer(k)], into.at[me], send.at[k], recv.at[me], "tensor", peer(k))

    @pl.loop(0, wk.shape[0] // TILE)
    def _(i):
        part = contract_cols(kg[...], wk[tile(i), :]) + contract_cols(vg[...], wv[tile(i), :])
        for p in range(blocks):
            terms[p, :, tile(i)] = part[p * R:(p + 1) * R].astype(BF)

    terms[blocks] = jnp.zeros_like(terms[0])

    @pl.loop(0, n)
    def _(k):
        for j in range(held):
            place = blocks
            for i in range(blocks):
                place = jnp.where(slot_at(i) == peer(k) * held + j, i, place)
            every[peer(k), j] = terms[place]

    @pl.loop(1, n)
    def _(k):
        scatter(every, n_in, ns_send, ns_recv, k).start()

    @pl.loop(0, heads)
    def _(lane):
        relay(0, lane)

    relay(0, heads)
    pass_on(extall, e_send, e_recv)

    def hidden_term(index):
        whole[index] = contract_cols(qgall[row], w[tile(index, depth), :]).astype(BF)

    @pl.loop(1, n)
    def _(k):
        hidden_term(peer(k))
        scatter(whole, h_in, hs_send, hs_recv, k).start()

    hidden_term(me)
    rest(extall, e_send, e_recv)
    mine.wait()

    def pick_copy(t):
        return pltpu.make_async_copy(
            extall.at[t, :, pl.ds(rows, share)], states.at[:, tile(t, share)], p_sem.at[t]
        )

    @pl.loop(0, n)
    def _(t):
        pick_copy(t).start()

    @pl.loop(0, n)
    def _(t):
        pick_copy(t).wait()

    for k in range(1, seqs):
        for lane, out in ((0, ogall), (1, qall)):
            z_came(out.at[over(k)], lane, over(k)).wait_recv()

    def add(origin, key_ref, value_ref):
        picks[...] = states[origin].T

        @pl.loop(0, width // TILE)
        def _(i):
            gk[:, tile(i)] += jnp.dot(picks[...], key_ref[:, tile(i)], preferred_element_type=F32)
            gv[:, tile(i)] += jnp.dot(picks[...], value_ref[:, tile(i)], preferred_element_type=F32)

    def rebuild(origin):
        @pl.loop(0, heads)
        def _(h):
            for lane, right, out in ((0, qall, keys), (1, ogall, values)):
                for u in range(spans):
                    here = pl.ds(u * SPAN, SPAN if u < spans - 1 else TAIL)
                    out[pl.ds(u * reach, reach), tile(h, HS)] = contract_rows(
                        zall[origin, h, lane, here, :], right[origin, here, tile(h, HS)]
                    ).astype(BF)

        add(origin, keys, values)

    gk[...] = jnp.zeros_like(gk)
    gv[...] = jnp.zeros_like(gv)
    add(row, kg, vg)
    for h in range(seqs - 1):
        if h > 0:
            @pl.loop(0, heads)
            def _(lane):
                relay(h, lane)

            relay(h, heads)
        for side in range(2):
            @pl.when(arrives(side, h))
            def _():
                rebuild(row - (1 - 2 * side) * (h + 1))

    for ref, into, send, recv, out in (
        (every, n_in, ns_send, ns_recv, nbr), (whole, h_in, hs_send, hs_recv, hid_out)
    ):
        @pl.loop(1, n)
        def _(k):
            remote(
                into.at[peer(k)], into.at[peer(k)], send.at[0], recv.at[peer(k)],
                "tensor", peer(k),
            ).wait_recv()

        into[me] = ref[me]
        total = into[0].astype(F32)
        for j in range(1, n):
            total = total + into[j].astype(F32)
        out[...] = total.astype(BF)

    for side in range(2):
        for h in range(seqs - 1):
            @pl.when(sends(side, h))
            def _():
                @pl.loop(0, heads)
                def _(lane):
                    hop(side, h, lane).wait_send()

                hop(side, h, heads).wait_send()

    sent(ext, extall, e_send, e_recv)
    for k in range(1, seqs):
        z_copy(ogall, 0, k).wait_send()
        z_copy(qall, 1, k).wait_send()

    @pl.loop(1, n)
    def _(k):
        scatter(whole, h_in, hs_send, hs_recv, k).wait_send()
        scatter(every, n_in, ns_send, ns_recv, k).wait_send()


def run(n, seqs, spans, slots, hid, nb, og, w_query, w_key, w_value):
    length, depth = hid.shape
    width = w_query.shape[1]
    heads = width // HS
    rows = (spans - 1) * SPAN + TAIL
    many = slots.shape[0] * slots.shape[1] * R
    cut, reach = DE // seqs, many // spans
    ext = (seqs, rows + many // n, cut)
    dma = pltpu.SemaphoreType.DMA

    def buf(*shape):
        return pltpu.VMEM(shape, BF)

    return pl.pallas_call(
        functools.partial(kernel, n, seqs, spans),
        out_shape=(
            jax.ShapeDtypeStruct((rows, width), BF),
            jax.ShapeDtypeStruct((rows, depth), BF),
            jax.ShapeDtypeStruct(nb.shape, BF),
            jax.ShapeDtypeStruct((seqs, rows, width), BF),
            jax.ShapeDtypeStruct((n,) + ext, BF),
            jax.ShapeDtypeStruct((cut, width), F32),
            jax.ShapeDtypeStruct((cut, width), F32),
        ),
        in_specs=[pl.BlockSpec(memory_space=pltpu.SMEM), VMEM, VMEM, VMEM, ANY, ANY, ANY],
        out_specs=(VMEM, VMEM, VMEM, VMEM, ANY, VMEM, VMEM),
        scratch_shapes=[
            buf(*w_query.shape), buf(*w_key.shape), buf(*w_value.shape),
            pltpu.VMEM((rows, width), F32),
            buf(rows, depth), buf(n, rows, depth), buf(n, *nb.shape), buf(seqs, many, cut),
            buf(many, width), buf(many, width), buf(many, width), buf(many, width),
            buf(seqs, rows, width), buf(seqs, rows, width), buf(*ext),
            buf(n, rows, depth), buf(n, *nb.shape), buf(many // R + 1, R, DE),
            buf(seqs, heads, 2, rows, reach), buf(cut, many),
            dma((3,)), dma((n + 1,)),
            dma((n,)), dma((n,)), dma((n,)), dma((n,)), dma((4, seqs)), dma((4, seqs)),
            dma((n,)), dma((n,)), dma((n,)), dma((n,)), dma((n,)), dma((n,)),
            dma((2, seqs - 1, heads + 1)), dma((2, seqs - 1, heads + 1)),
        ],
        compiler_params=pltpu.CompilerParams(
            collective_id=0, has_side_effects=True, vmem_limit_bytes=LIMIT
        ),
        name="fused",
    )(slots, hid, nb, og, w_query, w_key, w_value)


def body(n, seqs, hidden, neighbours, slot_of, w_query, w_key, w_value, out_grad):
    width = w_query.shape[1]
    length = hidden.shape[1]
    spans = slot_of.shape[1]
    lag = SPAN - 1
    mixed, hid, nbr, qgall, extall, wk, wv = run(
        n, seqs, spans, slot_of[0], hidden[0], neighbours[0], out_grad[0],
        w_query, w_key, w_value,
    )
    rows = mixed.shape[0]

    def back(x):
        return jnp.pad(x[: length - lag], ((lag, 0), (0, 0)))[None]

    pieces = w_query.shape[0] // seqs // extall.shape[3]
    query_part = lax.dot_general(
        extall[:pieces, :, :rows].transpose(0, 3, 1, 2).reshape(-1, seqs * rows),
        qgall.reshape(seqs * rows, width),
        (((1,), (0,)), ((), ())),
        preferred_element_type=F32,
    )
    return (back(mixed), back(hid), nbr[None], query_part, wk, wv)


def solution(mesh):
    return jax.shard_map(
        functools.partial(body, mesh.shape["tensor"], mesh.shape["seq"]),
        mesh=mesh,
        in_specs=(
            P("seq", None, "tensor"),
            P("seq", "tensor", None, None),
            P("seq", None, None),
            P(None, "tensor"),
            P(None, "tensor"),
            P(None, "tensor"),
            P("seq", None, "tensor"),
        ),
        out_specs=(
            P("seq", None, "tensor"),
            P("seq", None, "tensor"),
            P("seq", "tensor", None, None),
            P("seq", "tensor"),
            P("seq", "tensor"),
            P("seq", "tensor"),
        ),
        check_vma=False,
    )
```

time: 291 us -> 123 us (0.42)
  waiting for transfers between devices: 135 us -> 0 us
  Pallas kernels: 0 us -> 109 us
  matrix products: 55.2 us -> 5.78 us
  blocking collectives: 40 us -> 0 us
  local copies, waits for them, and re-layouts: 40.3 us -> 7.91 us
  between operations: 14.1 us -> 0.7 us
  starting transfers between devices: 4.64 us -> 0 us
    pallas_call x0 -> x1, Pallas kernels: none -> 109 us  [run(): pl.pallas_call(functools.partial(kernel, n, seqs, spans), out_shape=(jax....]
    reduce_scatter x2 -> x0, waiting for transfers between devices: 88.6 us -> none  [the longest x1 77.2 us: body(): lax.psum_scatter(both.astype(jnp.bfloat16), 'seq', scatter_dimension=0, t...]
    dot_general x15 -> x1, matrix products: 55.2 us -> 5.78 us  [body(): lax.dot_general(extall[:pieces, :, :rows].transpose(0, 3, 1, 2).reshape(-...]
    all_gather x2 -> x0, waiting for transfers between devices: 45.2 us -> none  [the longest x1 24.7 us: body(): whole = lax.all_gather(hidden[0, first:], 'tensor', axis=1, tiled=True)]
    all_gather x1 -> x0, blocking collectives: 40 us -> none  [body(): grads_all = lax.all_gather(query_grad, 'seq', axis=0, tiled=True)]
    unnamed x43 -> x12, local copies, waits for them, and re-layouts: 19.1 us -> 3.06 us
    all_to_all x1 -> x0, starting transfers between devices: 4.44 us -> none  [body(): lax.all_to_all(whole, 'seq', split_axis=1, concat_axis=0, tiled=True)]
    convert_element_type x4 -> x0, local copies, waits for them, and re-layouts: 4.41 us -> none  [the longest x1 2.61 us: body(): value_grad = jnp.einsum('uhqk,uqhd->ukhd', share_bf, grads, preferred_ele...]
  transfers between devices with their start and end apart: 6 -> 0, of which waited for: 4 -> 0; matrix products, arithmetic and copies ran while one was open for 19% -> 0% of each run, Pallas kernels for 0% -> 0%
where the time goes in v4:
time: 123 us
  Pallas kernels  109 us (89%)
  local copies, waits for them, and re-layouts  7.91 us (6%)
  matrix products  5.78 us (5%)
    pallas_call x1, Pallas kernels, run(): pl.pallas_call(functools.partial(kernel, n, seqs, spans), out_shape=(jax....  109 us
    dot_general x1, matrix products, body(): lax.dot_general(extall[:pieces, :, :rows].transpose(0, 3, 1, 2).reshape(-...  5.78 us
    unnamed x12, local copies, waits for them, and re-layouts  3.06 us

profile of v4, /device:TPU:0, one launch (start us, length us, event | category | flops | bytes accessed | tf_op | source)
XLA Modules:
  0.0 123.0 jit_solution(14479447300602892182)
XLA Ops:
  0.6 108.6 %fused.1 = (bf16[80,1024]{1,0:T(8,128)(2,1)}, bf16[80,1024]{1,0:T(8,128)(2,1)}, bf16[1,128,1024]{2,1,0:T(8,128)(2,1)}, bf16[4,80,1024]{2,1,0:T(8,128)(2,1)}, bf1...) custom-call(s32[2,2]{1,0:T(2,128)} %bitcast.26, bf16[128,1024]{1,0:T(8,128)(2,1)} %bitcast.22, ...), custom_call_target="tpu_custom_call" | custom-call | tf_op jit(solution)/shard_map/fused/pallas_call | solution.py:454
  109.3 0.9 slice.9
  110.2 0.9 slice.10
  111.1 0.9 pad_bitcast_fusion
  112.0 1.4 %slice_bitcast_fusion = bf16[8,256,4,80]{1,3,2,0:T(8,128)(2,1)S(1)} fusion(bf16[8,4,144,256]{3,2,1,0:T(8,128)(2,1)} %get-tuple-element.16), kind=kLoop, calls=%fused_computation | loop fusion | bytes 2621440 | tf_op jit(solution)/shard_map/transpose | solution.py:503
  113.4 0.0 copy-start.2
  113.4 0.7 copy.13
  114.2 0.4 copy.14
  114.6 0.0 copy-done.2
  114.6 0.0 copy-start.3
  114.6 0.0 copy-start.1
  114.6 5.8 %fusion = f32[2048,1024]{1,0:T(8,128)} fusion(bf16[2048,320]{0,1:T(8,128)(2,1)S(1)} %bitcast.19, bf16[320,1024]{1,0:T(8,128)(2,1)S(1)} %bitcast.21), kind=kOutput, calls=%fused_computation.3 | convolution fusion | flops 1342177280 | bytes 10354688 | tf_op jit(solution)/shard_map/dot_general | solution.py:502
  120.4 0.0 copy-done.3
  120.4 0.0 copy-start
  120.4 0.7 copy.18
  121.1 0.0 copy-done.1
  121.1 1.0 copy.19
  122.1 0.0 copy-done
  122.1 1.0 copy.20
Async XLA Ops:
  113.4 1.2 copy-start.2
  114.6 5.8 %copy-start.3 = (bf16[1,128,1024]{2,1,0:T(8,128)(2,1)S(1)}, bf16[1,128,1024]{2,1,0:T(8,128)(2,1)}, u32[]{:S(2)}) copy-start(bf16[1,128,1024]{2,1,0:T(8,128)(2,1)} %get-tuple-element.15) | copy-start | bytes 786436
  114.6 6.5 %copy-start.1 = (f32[256,1024]{1,0:T(8,128)S(1)}, f32[256,1024]{1,0:T(8,128)}, u32[]{:S(2)}) copy-start(f32[256,1024]{1,0:T(8,128)} %get-tuple-element.32) | copy-start | bytes 3145732
  120.4 1.7 %copy-start = (f32[256,1024]{1,0:T(8,128)S(1)}, f32[256,1024]{1,0:T(8,128)}, u32[]{:S(2)}) copy-start(f32[256,1024]{1,0:T(8,128)} %get-tuple-element.33) | copy-start | bytes 3145732

commit v5 on v4

--- a/solution.py
+++ b/solution.py
@@ -41,7 +41,7 @@
     n, seqs, spans, slots, hid_in, nb, og_in, w_hbm, wk_hbm, wv_hbm,
     mixed, hid_out, nbr, qgall, extall, gk, gv,
     w, wk, wv, acc, hid, whole, every, states, keys, values, kg, vg, qall, ogall, ext,
-    h_in, n_in, terms, zall, picks,
+    h_in, n_in, terms, zall, zlast, last, picks,
     w_sem, p_sem, h_send, h_recv, n_send, n_recv, z_send, z_recv,
     e_send, e_recv, hs_send, hs_recv, ns_send, ns_recv, line_send, line_recv,
 ):
@@ -194,6 +194,8 @@
         ext[row, pl.ds(0, rows), :] = whole[block, :, cols]
 
     qall[row] = acc[...].astype(BF)
+    for k in range(1, seqs):
+        z_copy(qall, 1, k).start()
     pass_on(every, n_send, n_recv)
     rest(every, n_send, n_recv)
     for i in range(blocks):
@@ -203,8 +205,6 @@
             states[part, pl.ds(i * R, R), :] = block[:, part * cut:(part + 1) * cut]
     for k in range(1, seqs):
         state_copy(k).start()
-    for k in range(1, seqs):
-        z_copy(qall, 1, k).start()
     ext[row, pl.ds(rows, share), :] = states[row, tile(me, share), :]
     for fetch in fetches[1:]:
         fetch.wait()
@@ -221,8 +221,8 @@
             out[:, tile(i)] = total.astype(BF)
 
     def lane_ref(origin, lane):
-        if isinstance(lane, int) and lane == heads:
-            return qgall.at[origin]
+        if isinstance(lane, int):
+            return (zlast if lane == heads else qgall).at[origin]
         return zall.at[origin, lane]
 
     def hop(side, h, lane):
@@ -263,6 +263,9 @@
                 @pl.when(sends(side, h + 1))
                 def _():
                     hop(side, h + 1, lane).start()
+
+    token = lax.broadcasted_iota(jnp.int32, last.shape[1:], 0)
+    last[...] = jnp.zeros_like(last)
 
     @pl.loop(0, heads)
     def _(h):
@@ -284,11 +287,16 @@
             ).astype(BF)
             kg[tall, at] = contract_rows(score_grad, qu).astype(BF)
             vg[tall, at] = contract_rows(share_bf, gu).astype(BF)
-            zall[row, h, 0, here, :] = score_grad
-            zall[row, h, 1, here, :] = share_bf
+            for lane, kept in ((0, score_grad), (1, share_bf)):
+                if u < spans - 1:
+                    zall[row, h, lane, here, :] = kept
+                else:
+                    last[lane] += jnp.where(token == h, kept.astype(F32)[0:1], 0.0)
         push(h)
 
+    zlast[row] = last[...].astype(BF)
     push(heads)
+    push(heads + 1)
 
     for k in range(1, seqs):
         came = over(k)
@@ -335,6 +343,7 @@
         relay(0, lane)
 
     relay(0, heads)
+    relay(0, heads + 1)
     pass_on(extall, e_send, e_recv)
 
     def hidden_term(index):
@@ -374,32 +383,62 @@
             gk[:, tile(i)] += jnp.dot(picks[...], key_ref[:, tile(i)], preferred_element_type=F32)
             gv[:, tile(i)] += jnp.dot(picks[...], value_ref[:, tile(i)], preferred_element_type=F32)
 
-    def rebuild(origin):
+    operands = ((0, qall, keys), (1, ogall, values))
+
+    def rebuild_head(origin, h):
+        at = tile(h, HS)
+        for lane, right, out in operands:
+            for u in range(spans - 1):
+                here = pl.ds(u * SPAN, SPAN)
+                out[pl.ds(u * reach, reach), at] = contract_rows(
+                    zall[origin, h, lane, here, :], right[origin, here, at]
+                ).astype(BF)
+
+    def rebuild_last(origin):
         @pl.loop(0, heads)
         def _(h):
-            for lane, right, out in ((0, qall, keys), (1, ogall, values)):
-                for u in range(spans):
-                    here = pl.ds(u * SPAN, SPAN if u < spans - 1 else TAIL)
-                    out[pl.ds(u * reach, reach), tile(h, HS)] = contract_rows(
-                        zall[origin, h, lane, here, :], right[origin, here, tile(h, HS)]
-                    ).astype(BF)
-
-        add(origin, keys, values)
+            at = tile(h, HS)
+            for lane, right, out in operands:
+                mine_only = jnp.where(token == h, zlast[origin, lane].astype(F32), 0.0).astype(BF)
+                only = right[origin, pl.ds((spans - 1) * SPAN, TAIL), at].astype(F32)
+                only = jnp.sum(only, axis=0, keepdims=True)
+                only = jnp.broadcast_to(only, (TAIL, HS)).astype(BF)
+                out[pl.ds((spans - 1) * reach, reach), at] = contract_rows(
+                    mine_only, only
+                ).astype(BF)
 
     gk[...] = jnp.zeros_like(gk)
     gv[...] = jnp.zeros_like(gv)
     add(row, kg, vg)
     for h in range(seqs - 1):
+        final = h == seqs - 2
+        origins = [row - (1 - 2 * side) * (h + 1) for side in range(2)]
         if h > 0:
             @pl.loop(0, heads)
             def _(lane):
                 relay(h, lane)
+                if final:
+                    for side in range(2):
+                        @pl.when(arrives(side, h))
+                        def _():
+                            rebuild_head(origins[side], lane)
 
             relay(h, heads)
+            if not final:
+                relay(h, heads + 1)
         for side in range(2):
             @pl.when(arrives(side, h))
             def _():
-                rebuild(row - (1 - 2 * side) * (h + 1))
+                if not (final and h > 0):
+                    @pl.loop(0, heads)
+                    def _(lane):
+                        rebuild_head(origins[side], lane)
+
+                rebuild_last(origins[side])
+                add(origins[side], keys, values)
+
+        if final and h > 0:
+            relay(h, heads + 1)
 
     for ref, into, send, recv, out in (
         (every, n_in, ns_send, ns_recv, nbr), (whole, h_in, hs_send, hs_recv, hid_out)
@@ -426,6 +465,7 @@
                     hop(side, h, lane).wait_send()
 
                 hop(side, h, heads).wait_send()
+                hop(side, h, heads + 1).wait_send()
 
     sent(ext, extall, e_send, e_recv)
     for k in range(1, seqs):
@@ -471,11 +511,12 @@
             buf(many, width), buf(many, width), buf(many, width), buf(many, width),
             buf(seqs, rows, width), buf(seqs, rows, width), buf(*ext),
             buf(n, rows, depth), buf(n, *nb.shape), buf(many // R + 1, R, DE),
-            buf(seqs, heads, 2, rows, reach), buf(cut, many),
+            buf(seqs, heads, 2, rows - TAIL, reach), buf(seqs, 2, TAIL, reach),
+            pltpu.VMEM((2, TAIL, reach), F32), buf(cut, many),
             dma((3,)), dma((n + 1,)),
             dma((n,)), dma((n,)), dma((n,)), dma((n,)), dma((4, seqs)), dma((4, seqs)),
             dma((n,)), dma((n,)), dma((n,)), dma((n,)), dma((n,)), dma((n,)),
-            dma((2, seqs - 1, heads + 1)), dma((2, seqs - 1, heads + 1)),
+            dma((2, seqs - 1, heads + 2)), dma((2, seqs - 1, heads + 2)),
         ],
         compiler_params=pltpu.CompilerParams(
             collective_id=0, has_side_effects=True, vmem_limit_bytes=LIMIT

time: 123 us -> 120 us (0.976)
  Pallas kernels: 109 us -> 105 us
    pallas_call x1, Pallas kernels: 109 us -> 105 us  [run(): pl.pallas_call(functools.partial(kernel, n, seqs, spans), out_shape=(jax....]
where the time goes in v5:
time: 120 us
  Pallas kernels  105 us (88%)
  local copies, waits for them, and re-layouts  7.91 us (7%)
  matrix products  5.78 us (5%)
    pallas_call x1, Pallas kernels, run(): pl.pallas_call(functools.partial(kernel, n, seqs, spans), out_shape=(jax....  105 us
    dot_general x1, matrix products, body(): lax.dot_general(extall[:pieces, :, :rows].transpose(0, 3, 1, 2).reshape(-...  5.78 us
    unnamed x12, local copies, waits for them, and re-layouts  3.06 us

profile of v5, /device:TPU:0, one launch (start us, length us, event | category | flops | bytes accessed | tf_op | source)
XLA Modules:
  0.0 119.5 jit_solution(16299832004887098557)
XLA Ops:
  0.6 105.1 %fused.1 = (bf16[80,1024]{1,0:T(8,128)(2,1)}, bf16[80,1024]{1,0:T(8,128)(2,1)}, bf16[1,128,1024]{2,1,0:T(8,128)(2,1)}, bf16[4,80,1024]{2,1,0:T(8,128)(2,1)}, bf1...) custom-call(s32[2,2]{1,0:T(2,128)} %bitcast.26, bf16[128,1024]{1,0:T(8,128)(2,1)} %bitcast.22, ...), custom_call_target="tpu_custom_call" | custom-call | tf_op jit(solution)/shard_map/fused/pallas_call | solution.py:494
  105.8 0.9 slice.9
  106.7 0.9 slice.10
  107.6 0.9 pad_bitcast_fusion
  108.5 1.4 %slice_bitcast_fusion = bf16[8,256,4,80]{1,3,2,0:T(8,128)(2,1)S(1)} fusion(bf16[8,4,144,256]{3,2,1,0:T(8,128)(2,1)} %get-tuple-element.16), kind=kLoop, calls=%fused_computation | loop fusion | bytes 2621440 | tf_op jit(solution)/shard_map/transpose | solution.py:544
  109.9 0.0 copy-start.2
  109.9 0.7 copy.13
  110.6 0.4 copy.14
  111.0 0.0 copy-done.2
  111.1 0.0 copy-start.3
  111.1 0.0 copy-start.1
  111.1 5.8 %fusion = f32[2048,1024]{1,0:T(8,128)} fusion(bf16[2048,320]{0,1:T(8,128)(2,1)S(1)} %bitcast.19, bf16[320,1024]{1,0:T(8,128)(2,1)S(1)} %bitcast.21), kind=kOutput, calls=%fused_computation.3 | convolution fusion | flops 1342177280 | bytes 10354688 | tf_op jit(solution)/shard_map/dot_general | solution.py:543
  116.9 0.0 copy-done.3
  116.9 0.0 copy-start
  116.9 0.7 copy.18
  117.6 0.0 copy-done.1
  117.6 1.0 copy.19
  118.5 0.0 copy-done
  118.5 1.0 copy.20
Async XLA Ops:
  109.9 1.2 copy-start.2
  111.1 5.8 %copy-start.3 = (bf16[1,128,1024]{2,1,0:T(8,128)(2,1)S(1)}, bf16[1,128,1024]{2,1,0:T(8,128)(2,1)}, u32[]{:S(2)}) copy-start(bf16[1,128,1024]{2,1,0:T(8,128)(2,1)} %get-tuple-element.15) | copy-start | bytes 786436
  111.1 6.5 %copy-start.1 = (f32[256,1024]{1,0:T(8,128)S(1)}, f32[256,1024]{1,0:T(8,128)}, u32[]{:S(2)}) copy-start(f32[256,1024]{1,0:T(8,128)} %get-tuple-element.32) | copy-start | bytes 3145732
  116.9 1.7 %copy-start = (f32[256,1024]{1,0:T(8,128)S(1)}, f32[256,1024]{1,0:T(8,128)}, u32[]{:S(2)}) copy-start(f32[256,1024]{1,0:T(8,128)} %get-tuple-element.33) | copy-start | bytes 3145732

commit v6 on v5

--- a/solution.py
+++ b/solution.py
@@ -413,19 +413,16 @@
     for h in range(seqs - 1):
         final = h == seqs - 2
         origins = [row - (1 - 2 * side) * (h + 1) for side in range(2)]
-        if h > 0:
+        if final and h > 0:
             @pl.loop(0, heads)
             def _(lane):
                 relay(h, lane)
-                if final:
-                    for side in range(2):
-                        @pl.when(arrives(side, h))
-                        def _():
-                            rebuild_head(origins[side], lane)
+                for side in range(2):
+                    @pl.when(arrives(side, h))
+                    def _():
+                        rebuild_head(origins[side], lane)
 
             relay(h, heads)
-            if not final:
-                relay(h, heads + 1)
         for side in range(2):
             @pl.when(arrives(side, h))
             def _():
@@ -436,6 +433,14 @@
 
                 rebuild_last(origins[side])
                 add(origins[side], keys, values)
+
+            if side == 0 and h + 1 < seqs - 2:
+                @pl.loop(0, heads)
+                def _(lane):
+                    relay(h + 1, lane)
+
+                relay(h + 1, heads)
+                relay(h + 1, heads + 1)
 
         if final and h > 0:
             relay(h, heads + 1)

time: 120 us -> 115 us (0.958)
  Pallas kernels: 105 us -> 100 us
    pallas_call x1, Pallas kernels: 105 us -> 100 us  [run(): pl.pallas_call(functools.partial(kernel, n, seqs, spans), out_shape=(jax....]
where the time goes in v6:
time: 115 us
  Pallas kernels  100 us (87%)
  local copies, waits for them, and re-layouts  7.91 us (7%)
  matrix products  5.78 us (5%)
    pallas_call x1, Pallas kernels, run(): pl.pallas_call(functools.partial(kernel, n, seqs, spans), out_shape=(jax....  100 us
    dot_general x1, matrix products, body(): lax.dot_general(extall[:pieces, :, :rows].transpose(0, 3, 1, 2).reshape(-...  5.78 us
    unnamed x12, local copies, waits for them, and re-layouts  3.06 us

profile of v6, /device:TPU:0, one launch (start us, length us, event | category | flops | bytes accessed | tf_op | source)
XLA Modules:
  0.0 114.5 jit_solution(7966027205075908192)
XLA Ops:
  0.6 100.1 %fused.1 = (bf16[80,1024]{1,0:T(8,128)(2,1)}, bf16[80,1024]{1,0:T(8,128)(2,1)}, bf16[1,128,1024]{2,1,0:T(8,128)(2,1)}, bf16[4,80,1024]{2,1,0:T(8,128)(2,1)}, bf1...) custom-call(s32[2,2]{1,0:T(2,128)} %bitcast.26, bf16[128,1024]{1,0:T(8,128)(2,1)} %bitcast.22, ...), custom_call_target="tpu_custom_call" | custom-call | tf_op jit(solution)/shard_map/fused/pallas_call | solution.py:499
  100.8 0.9 slice.9
  101.7 0.9 slice.10
  102.6 0.9 pad_bitcast_fusion
  103.5 1.4 %slice_bitcast_fusion = bf16[8,256,4,80]{1,3,2,0:T(8,128)(2,1)S(1)} fusion(bf16[8,4,144,256]{3,2,1,0:T(8,128)(2,1)} %get-tuple-element.16), kind=kLoop, calls=%fused_computation | loop fusion | bytes 2621440 | tf_op jit(solution)/shard_map/transpose | solution.py:549
  104.9 0.0 copy-start.2
  104.9 0.7 copy.13
  105.7 0.4 copy.14
  106.1 0.0 copy-done.2
  106.1 0.0 copy-start.3
  106.1 0.0 copy-start.1
  106.1 5.8 %fusion = f32[2048,1024]{1,0:T(8,128)} fusion(bf16[2048,320]{0,1:T(8,128)(2,1)S(1)} %bitcast.19, bf16[320,1024]{1,0:T(8,128)(2,1)S(1)} %bitcast.21), kind=kOutput, calls=%fused_computation.3 | convolution fusion | flops 1342177280 | bytes 10354688 | tf_op jit(solution)/shard_map/dot_general | solution.py:548
  111.9 0.0 copy-done.3
  111.9 0.0 copy-start
  111.9 0.7 copy.18
  112.6 0.0 copy-done.1
  112.6 1.0 copy.19
  113.6 0.0 copy-done
  113.6 1.0 copy.20
Async XLA Ops:
  104.9 1.2 %copy-start.2 = (bf16[4,80,1024]{2,1,0:T(8,128)(2,1)S(1)}, bf16[4,80,1024]{2,1,0:T(8,128)(2,1)}, u32[]{:S(2)}) copy-start(bf16[4,80,1024]{2,1,0:T(8,128)(2,1)} %get-tuple-element.17) | copy-start | bytes 1966084
  106.1 5.8 %copy-start.3 = (bf16[1,128,1024]{2,1,0:T(8,128)(2,1)S(1)}, bf16[1,128,1024]{2,1,0:T(8,128)(2,1)}, u32[]{:S(2)}) copy-start(bf16[1,128,1024]{2,1,0:T(8,128)(2,1)} %get-tuple-element.15) | copy-start | bytes 786436
  106.1 6.5 %copy-start.1 = (f32[256,1024]{1,0:T(8,128)S(1)}, f32[256,1024]{1,0:T(8,128)}, u32[]{:S(2)}) copy-start(f32[256,1024]{1,0:T(8,128)} %get-tuple-element.32) | copy-start | bytes 3145732
  111.9 1.7 %copy-start = (f32[256,1024]{1,0:T(8,128)S(1)}, f32[256,1024]{1,0:T(8,128)}, u32[]{:S(2)}) copy-start(f32[256,1024]{1,0:T(8,128)} %get-tuple-element.33) | copy-start | bytes 3145732
